TPU v7x, 256 devices: a whole 4x4x8 slice. The times are simulated.
256 devices in a mesh: leaf: 64 (over y_hi, z, x), rank: 4 (over y_lo, core).
Axes of the slice: x: 4, y: 4 (y_hi: 2, y_lo: 2; y = y_hi * 2 + y_lo), z: 8, core: 2. Of those that a mesh axis runs over, the one named last changes fastest.
Arguments:
- vectors: bfloat16 [4096, 64, 64], P('leaf'), may hold values from -6 to 6
- near_blocks: bfloat16 [4096, 32, 64, 64], P('leaf', 'rank'), may hold values from -0.125 to 0.125
- near_offsets: int32 [4096, 32], P('leaf', 'rank'), may hold values from -64 to 64
- near_count: int32 [4096], P('leaf'), may hold values from 1 to 32
- basis: bfloat16 [4096, 64, 64], P('leaf'), may hold values from -0.75 to 0.75
- child_transfer: bfloat16 [4096, 64, 64], P('leaf'), may hold values from -0.25 to 0.25
- parent_transfer: bfloat16 [512, 64, 64], P('leaf'), may hold values from -0.25 to 0.25
- leaf_coupling: bfloat16 [4096, 32, 64, 64], P('leaf', 'rank'), may hold values from -0.125 to 0.125
- leaf_offsets: int32 [4096, 32], P('leaf', 'rank'), may hold values from -64 to 64
- top_coupling: bfloat16 [64, 16, 64, 64], P('leaf', 'rank'), may hold values from -0.1875 to 0.1875
- top_ids: int32 [64, 16], P('leaf', 'rank'), may hold values from 0 to 63
Outputs:
- product: bfloat16 [4096, 64, 64], P('leaf', 'rank')
All inputs are finite; a program needn't handle non-finite values.
Results may differ from a plain program's by a relative error of at most 0.015.
Values may be sent and summed in bfloat16 or wider, within the bound.
No kernel may reach another device: no remote copies, remote signals or barrier semaphores. Data moves between devices by JAX's collectives and lax.ppermute only.
A program may use at most 128 MiB of HBM per device.

v0:
```python
import jax
import jax.numpy as jnp
from jax import lax
from jax.sharding import PartitionSpec as P


def with_halo(block, sides, width):
    for axis, dim in sides:
        count = lax.axis_size(axis)
        forward = [(i, i + 1) for i in range(count - 1)]
        backward = [(target, source) for source, target in forward]
        low = lax.ppermute(
            lax.slice_in_dim(block, block.shape[dim] - width, None, axis=dim), axis, forward
        )
        high = lax.ppermute(lax.slice_in_dim(block, 0, width, axis=dim), axis, backward)
        block = jnp.concatenate([low, block, high], axis=dim)
    return block


def descend(top_terms, leaf_terms, parent_transfer, child_transfer):
    highest = lax.Precision.HIGHEST
    middle_terms = jnp.einsum(
        "mjk,mkr->mjr",
        parent_transfer.astype(jnp.float32),
        jnp.repeat(top_terms, 8, axis=0),
        precision=highest,
    )
    return leaf_terms + jnp.einsum(
        "ljk,lkr->ljr",
        child_transfer.astype(jnp.float32),
        jnp.repeat(middle_terms, 8, axis=0),
        precision=highest,
    )


def shards(
    vectors,
    near_blocks,
    near_offsets,
    near_count,
    basis,
    child_transfer,
    parent_transfer,
    leaf_coupling,
    leaf_offsets,
    top_coupling,
    top_ids,
):
    highest = lax.Precision.HIGHEST
    leaf_dev = vectors.shape[0]
    points = vectors.shape[1]
    columns = vectors.shape[2]
    rank_width = basis.shape[2]
    total_leaves = leaf_dev * lax.axis_size("leaf")
    own_first = lax.axis_index("leaf") * leaf_dev
    rank_pos = lax.axis_index("rank")
    local_ids = own_first + jnp.arange(leaf_dev, dtype=jnp.int32)
    moments = jnp.einsum("lpk,lpr->lkr", basis, vectors, preferred_element_type=jnp.float32).astype(
        jnp.bfloat16
    )
    extended = with_halo(vectors, (("leaf", 0),), leaf_dev)
    moment_ext = with_halo(moments, (("leaf", 0),), leaf_dev)
    near_slots = near_offsets.shape[1]
    near_index = (
        jnp.clip(local_ids[:, None] + near_offsets, 0, total_leaves - 1) - own_first + leaf_dev
    )
    fetched = extended[near_index]
    slot_ids = rank_pos * near_slots + jnp.arange(near_slots, dtype=jnp.int32)
    live_slots = slot_ids[None, :] < near_count[:, None]
    fetched = jnp.where(live_slots[:, :, None, None], fetched, jnp.zeros((), jnp.bfloat16))
    near_part = jnp.einsum(
        "lspq,lsqr->lpr", near_blocks, fetched, preferred_element_type=jnp.float32
    )
    leaf_index = (
        jnp.clip(local_ids[:, None] + leaf_offsets, 0, total_leaves - 1) - own_first + leaf_dev
    )
    picked = moment_ext[leaf_index]
    leaf_part = jnp.einsum(
        "lsjk,lskr->ljr", leaf_coupling, picked, preferred_element_type=jnp.float32
    )
    middle = jnp.einsum("lkj,lkr->ljr", child_transfer, moments, preferred_element_type=jnp.float32)
    middle = middle.reshape(leaf_dev // 8, 8, rank_width, columns).sum(1).astype(jnp.bfloat16)
    upper = jnp.einsum("mkj,mkr->mjr", parent_transfer, middle, preferred_element_type=jnp.float32)
    upper = upper.reshape(leaf_dev // 64, 8, rank_width, columns).sum(1).astype(jnp.bfloat16)
    shard_piece = lax.all_gather(upper, "leaf", axis=0, tiled=True)
    piece_count = shard_piece.shape[0]
    select = (top_ids[:, :, None] == jnp.arange(piece_count, dtype=jnp.int32)).astype(jnp.bfloat16)
    chosen = jnp.einsum(
        "tsn,nkr->tskr", select, shard_piece, preferred_element_type=jnp.float32
    ).astype(jnp.bfloat16)
    top_part = jnp.einsum(
        "tsjk,tskr->tjr", top_coupling, chosen, preferred_element_type=jnp.float32
    )
    piece_rows = points // lax.axis_size("rank")
    top_sum, leaf_sum = (
        lax.psum(top_part.astype(jnp.bfloat16), "rank").astype(jnp.float32),
        lax.psum(leaf_part.astype(jnp.bfloat16), "rank").astype(jnp.float32),
    )
    leaf_field = descend(top_sum, leaf_sum, parent_transfer, child_transfer)
    basis_rows = lax.dynamic_slice_in_dim(basis, rank_pos * piece_rows, piece_rows, 1)
    far_field = jnp.einsum(
        "lpk,lkr->lpr", basis_rows.astype(jnp.float32), leaf_field, precision=highest
    )
    result = (
        lax.psum_scatter(
            near_part.astype(jnp.bfloat16), "rank", scatter_dimension=1, tiled=True
        ).astype(jnp.float32)
        + far_field
    )
    return result.astype(jnp.bfloat16)


def solution(mesh):
    in_specs = (
        P("leaf", None, None),
        P("leaf", "rank", None, None),
        P("leaf", "rank"),
        P("leaf"),
        P("leaf", None, None),
        P("leaf", None, None),
        P("leaf", None, None),
        P("leaf", "rank", None, None),
        P("leaf", "rank"),
        P("leaf", "rank", None, None),
        P("leaf", "rank"),
    )
    out_specs = P("leaf", "rank", None)
    return jax.shard_map(shards, mesh=mesh, in_specs=in_specs, out_specs=out_specs, check_vma=False)
```

profile of v0, /device:TPU:1, one launch (start us, length us, event | category | flops | bytes accessed | tf_op | source)
XLA Modules:
  0.0 357.8 jit_solution(17153096425128031131)
XLA Ops:
  6.6 1.2 copy-done
  7.8 1.7 convolution_convert_fusion
  9.5 5.0 %collective-permute-start.2 = (bf16[64,64,64]{2,1,0:T(8,128)(2,1)S(1)}, bf16[64,64,64]{2,1,0:T(8,128)(2,1)}, u32[]{:S(2)}, u32[]{:S(2)}) collective-permute-start(bf16[64,64,64]{2,1,0:T(8,128)(2,1)S(1)} %convolution_convert_fusion), channel_id=1, source_target_pairs={{0,4},{4,8},{8,12},{12,16},{16,20},{20,24},{24,28},{28,32},{32,36}... | collective-permute-start | bytes 1572872 | tf_op jit(solution)/shard_map/ppermute | solution.py:12
  14.5 1.3 collective-permute-start.3
  15.8 5.0 %collective-permute-start = (bf16[64,64,64]{2,1,0:T(8,128)(2,1)}, bf16[64,64,64]{2,1,0:T(8,128)(2,1)}, u32[]{:S(2)}, u32[]{:S(2)}) collective-permute-start(bf16[64,64,64]{2,1,0:T(8,128)(2,1)} %param.11), channel_id=1, source_target_pairs={{0,4},{4,8},{8,12},{12,16},{16,20},{20,24},{24,28},{28,32},{32,36}... | collective-permute-start | bytes 1572872 | tf_op jit(solution)/shard_map/ppermute | solution.py:12
  20.8 1.3 collective-permute-start.1
  22.2 0.1 copy.42
  22.2 0.1 reshape.94
  22.3 0.1 copy.37
  22.4 0.1 reshape.86
  22.5 0.5 bitcast_reduce_fusion
  23.1 0.2 fusion.17
  23.3 0.1 copy.45
  23.4 0.1 broadcast_compare_fusion
  23.5 189.5 %all-gather = bf16[4096,64]{1,0:T(8,128)(2,1)S(1)} all-gather(bf16[64,64]{1,0:T(8,128)(2,1)S(1)} %copy.45), channel_id=2, replica_groups=mesh['leaf'=64,'rank'=4] {'leaf'}, dimensions={0}, use_global_device_ids=true | all-gather | bytes 532480 | tf_op jit(solution)/shard_map/all_gather | solution.py:85
  213.0 3.3 pad_maximum_fusion.1
  216.3 21.5 %gather_fusion.1 = bf16[512,64,64]{2,1,0:T(8,128)(2,1)} fusion(bf16[192,64,64]{2,1,0:T(8,128)(2,1)} %pad_maximum_fusion.1, s32[1024]{0:T(1024)S(1)} %pad_clamp_fusion), kind=kCustom, calls=%fused_computation.1 | custom fusion | bytes 8390656 | tf_op jit(solution)/shard_map/gather | solution.py:77
  237.9 9.2 %fusion.8 = bf16[64,64,64]{1,2,0:T(8,128)(2,1)} fusion(bf16[64,8,64,64]{3,2,1,0:T(8,128)(2,1)} %bitcast.66, bf16[64,8,64,64]{3,2,1,0:T(8,128)(2,1)} %param.18), kind=kOutput, calls=%fused_computation.15 | convolution fusion | flops 268697600 | bytes 8912896 | tf_op jit(solution)/shard_map/lsjk,lskr->ljr/dot_general | solution.py:78
  247.1 0.2 reduce-scatter.2.cloned.1.call-start
  247.3 3.5 pad_maximum_fusion
  250.8 21.5 %gather_fusion = bf16[512,64,64]{2,1,0:T(8,128)(2,1)} fusion(bf16[192,64,64]{2,1,0:T(8,128)(2,1)} %pad_maximum_fusion, s32[1024]{0:T(1024)S(1)} %pad_clamp_fusion.1), kind=kCustom, calls=%fused_computation | custom fusion | bytes 8390656 | tf_op jit(solution)/shard_map/gather | solution.py:67
  272.3 11.9 %copy.38 = bf16[64,8,64,64]{2,3,1,0:T(8,128)(2,1)} copy(bf16[64,8,64,64]{3,2,1,0:T(8,128)(2,1)} %bitcast.67) | data formatting | bytes 8388608 | tf_op jit(solution)/shard_map/gather | solution.py:67
  284.3 7.5 %fusion.9 = bf16[64,64,64]{1,2,0:T(8,128)(2,1)S(1)} fusion(bf16[64,8,64,64]{3,2,1,0:T(8,128)(2,1)} %param.12, bf16[64,8,64,64]{2,3,1,0:T(8,128)(2,1)} %copy.38, pred[64,8]{1,0:T(8,128)(4,1)S(1)} %broadcast_compare_fusion), kind=kOutput, calls=%fused_computation.16 | convolution fusion | flops 270794752 | bytes 8913408 | tf_op jit(solution)/shard_map/lspq,lsqr->lpr/dot_general | solution.py:71
  291.8 2.4 copy.39
  294.2 0.7 convolution_convert_fusion.1
  294.9 0.2 fusion.16
  295.1 36.2 %psum.15 = bf16[64,64]{0,1:T(8,128)(2,1)S(1)} all-reduce(bf16[64,64]{0,1:T(8,128)(2,1)S(1)} %fusion.16), channel_id=1, replica_groups=mesh['leaf'=64,'rank'=4] {'rank'}, use_global_device_ids=true, to_apply=%region_3.4 | all-reduce | flops 4096 | bytes 16384 | tf_op jit(solution)/shard_map/psum | solution.py:96
  331.3 0.3 convolution_bitcast_fusion
  331.6 0.2 broadcast_in_dim.33
  331.9 3.0 fusion.29
  334.9 12.3 %reduce-scatter.2.cloned.1.call-done = bf16[64,16,64]{2,0,1:T(8,128)(2,1)} async-done(((bf16[64,64,64]{2,0,1:T(8,128)(2,1)}), bf16[64,16,64]{2,0,1:T(8,128)(2,1)}) %reduce-scatter.2.cloned.1.call-update) | async-done | bytes 131088 | tf_op jit(solution)/shard_map/reduce_scatter | solution.py:105
  347.2 3.8 %fusion.13 = bf16[64,16,64]{2,1,0:T(8,128)(2,1)} fusion(f32[64,64,64]{2,1,0:T(8,128)S(1)} %fusion.29, bf16[64,64,64]{1,2,0:T(8,128)(2,1)} %all-reduce.2.cloned.1.call-done, bf16[64,16,64]{2,0,1:T(8,128)(2,1)} %reduce-scatter.2.cloned.1.call-done, bf16[64,64,64]{2,1,0:T(8,128)(2,1)S(1)} %copy-done, s32[]{:T(128)S(6)} %select_n.15), kind=kOutput, calls=%fused_computation.18 | convolution fusion | flops 51052544 | bytes 3145732 | tf_op jit(solution)/shard_map/lpk,lkr->lpr/dot_general | solution.py:101
  (29 shorter events, 0.2 us)
Async XLA Ops:
  6.5 1.2 copy-start
  6.5 15.6 %copy-start.4 = (s32[64,8]{0,1:T(8,128)S(1)}, s32[64,8]{0,1:T(8,128)}, u32[]{:S(2)}) copy-start(s32[64,8]{0,1:T(8,128)} %param.13) | copy-start | bytes 6148
  6.5 15.6 %copy-start.5 = (s32[64,8]{0,1:T(8,128)S(1)}, s32[64,8]{0,1:T(8,128)}, u32[]{:S(2)}) copy-start(s32[64,8]{0,1:T(8,128)} %param.19) | copy-start | bytes 6148
  6.5 16.0 %copy-start.1 = (bf16[64,64,64]{2,1,0:T(8,128)(2,1)S(1)}, bf16[64,64,64]{2,1,0:T(8,128)(2,1)}, u32[]{:S(2)}) copy-start(bf16[64,64,64]{2,1,0:T(8,128)(2,1)} %param.16) | copy-start | bytes 1572868
  6.5 16.5 %copy-start.2 = (bf16[8,64,64]{2,1,0:T(8,128)(2,1)S(1)}, bf16[8,64,64]{2,1,0:T(8,128)(2,1)}, u32[]{:S(2)}) copy-start(bf16[8,64,64]{2,1,0:T(8,128)(2,1)} %param.17) | copy-start | bytes 196612
  6.5 16.9 %copy-start.7 = (s32[64]{0:T(128)S(1)}, s32[64]{0:T(128)}, u32[]{:S(2)}) copy-start(s32[64]{0:T(128)} %param.14) | copy-start | bytes 772
  6.6 328.3 %all-reduce.2.cloned.1.call-start = ((), (), s32[]{:S(2)}) async-start(), calls=%async_computation.2 | async-start | bytes 2097152 | tf_op jit(solution)/shard_map/psum | solution.py:97
  9.5 203.5 %collective-permute-start.2 = (bf16[64,64,64]{2,1,0:T(8,128)(2,1)S(1)}, bf16[64,64,64]{2,1,0:T(8,128)(2,1)}, u32[]{:S(2)}, u32[]{:S(2)}) collective-permute-start(bf16[64,64,64]{2,1,0:T(8,128)(2,1)S(1)} %convolution_convert_fusion), channel_id=1, source_target_pairs={{0,4},{4,8},{8,12},{12,16},{16,20},{20,24},{24,28},{28,32},{32,36}... | collective-permute-start | bytes 1572872 | tf_op jit(solution)/shard_map/ppermute | solution.py:12
  14.5 198.5 %collective-permute-start.3 = (bf16[64,64,64]{2,1,0:T(8,128)(2,1)S(1)}, bf16[64,64,64]{2,1,0:T(8,128)(2,1)}, u32[]{:S(2)}, u32[]{:S(2)}) collective-permute-start(bf16[64,64,64]{2,1,0:T(8,128)(2,1)S(1)} %convolution_convert_fusion), channel_id=1, source_target_pairs={{4,0},{8,4},{12,8},{16,12},{20,16},{24,20},{28,24},{32,28},{36,32}... | collective-permute-start | bytes 1572872 | tf_op jit(solution)/shard_map/ppermute | solution.py:15
  15.8 231.5 %collective-permute-start = (bf16[64,64,64]{2,1,0:T(8,128)(2,1)}, bf16[64,64,64]{2,1,0:T(8,128)(2,1)}, u32[]{:S(2)}, u32[]{:S(2)}) collective-permute-start(bf16[64,64,64]{2,1,0:T(8,128)(2,1)} %param.11), channel_id=1, source_target_pairs={{0,4},{4,8},{8,12},{12,16},{16,20},{20,24},{24,28},{28,32},{32,36}... | collective-permute-start | bytes 1572872 | tf_op jit(solution)/shard_map/ppermute | solution.py:12
  20.8 226.5 %collective-permute-start.1 = (bf16[64,64,64]{2,1,0:T(8,128)(2,1)}, bf16[64,64,64]{2,1,0:T(8,128)(2,1)}, u32[]{:S(2)}, u32[]{:S(2)}) collective-permute-start(bf16[64,64,64]{2,1,0:T(8,128)(2,1)} %param.11), channel_id=1, source_target_pairs={{4,0},{8,4},{12,8},{16,12},{20,16},{24,20},{28,24},{32,28},{36,32}... | collective-permute-start | bytes 1572872 | tf_op jit(solution)/shard_map/ppermute | solution.py:15
  247.1 100.1 %reduce-scatter.2.cloned.1.call-start = ((), (), s32[]{:S(2)}) async-start(), calls=%async_computation.1 | async-start | bytes 1310720 | tf_op jit(solution)/shard_map/reduce_scatter | solution.py:105
  291.8 2.4 copy-start.6
  291.8 3.1 copy-start.3
Sparse Core Ops, SparseCore 0:
  247.2 73.4 all-reduce.1
  323.4 23.7 reduce-scatter.1
where the time goes:
time: 359 us; the launch traced here: 358 us
  blocking collectives  226 us (63%)
  local copies, waits for them, and re-layouts  59.2 us (16%)
  matrix products  27.2 us (8%)
  between operations  13.6 us (4%)
  starting transfers between devices  12.8 us (4%)
  waiting for transfers between devices  12.4 us (3%)
  other arithmetic  6.91 us (2%)
    all_gather x1, blocking collectives, shards(): shard_piece = lax.all_gather(upper, 'leaf', axis=0, tiled=True)  190 us
    psum x1, blocking collectives, shards(): lax.psum(top_part.astype(jnp.bfloat16), 'rank').astype(jnp.float32)  36.2 us
    gather x2, local copies, waits for them, and re-layouts, shards(): fetched = extended[near_index]  33.4 us
    gather x1, local copies, waits for them, and re-layouts, shards(): picked = moment_ext[leaf_index]  21.5 us
    reduce_scatter x1, waiting for transfers between devices, shards(): lax.psum_scatter(near_part.astype(jnp.bfloat16), 'rank', scatter_dimensio...  12.3 us
    ppermute x2, starting transfers between devices, with_halo(): lax.ppermute(lax.slice_in_dim(block, block.shape[dim] - width, None, axis...  10 us
    dot_general x1, matrix products, shards(): jnp.einsum('lsjk,lskr->ljr', leaf_coupling, picked, preferred_element_typ...  9.19 us
    dot_general x1, matrix products, shards(): jnp.einsum('lspq,lsqr->lpr', near_blocks, fetched, preferred_element_type...  7.54 us
  transfers between devices with their start and end apart: 6, of which 1 were waited for; matrix products, arithmetic and copies ran while one was open for 24% of the time, Pallas kernels for 0%

commit v1 on v0

v1 whole, which is shorter than its diff:
```python
import functools

import jax
import jax.numpy as jnp
from jax import lax
from jax.experimental import pallas as pl
from jax.experimental.pallas import tpu as pltpu
from jax.sharding import PartitionSpec as P

F32 = jnp.float32
BF16 = jnp.bfloat16
VMEM_LIMIT = 40 * 1024 * 1024
STEP = 8


def params():
    return pltpu.CompilerParams(vmem_limit_bytes=VMEM_LIMIT)


def dot(a, b):
    return jnp.dot(a, b, preferred_element_type=F32)


def dot_t(a, b):
    return lax.dot_general(a, b, (((0,), (0,)), ((), ())), preferred_element_type=F32)


def pack_kernel(v_ref, o_ref):
    half = o_ref.shape[0]
    o_ref[...] = jnp.concatenate([v_ref[:half], v_ref[half:]], axis=-1)


def pack(v):
    n, p, c = v.shape
    return pl.pallas_call(
        pack_kernel,
        out_shape=jax.ShapeDtypeStruct((n // 2, p, 2 * c), v.dtype),
        compiler_params=params(),
        name="pack_vectors",
    )(v)


def upward_kernel(v_ref, b_ref, c_ref, p_ref, mom_ref, up_ref, m_s, mid_s):
    n, k, c = m_s.shape
    half = n // 2
    for l in range(n):
        m_s[l] = dot_t(b_ref[l], v_ref[l]).astype(BF16)
    mom_ref[...] = jnp.concatenate([m_s[:half], m_s[half:]], axis=-1)
    for m in range(n // 8):
        child = c_ref[8 * m : 8 * m + 8].reshape(8 * k, k)
        mid_s[m] = dot_t(child, m_s[8 * m : 8 * m + 8].reshape(8 * k, c)).astype(BF16)
    up = dot_t(p_ref[...].reshape(8 * k, k), mid_s[...].reshape(8 * k, c)).astype(BF16)
    up_ref[...] = jnp.concatenate([up[: k // 2], up[k // 2 :]], axis=-1)


def upward(vectors, basis, child, parent):
    n, p, c = vectors.shape
    k = basis.shape[2]
    return pl.pallas_call(
        upward_kernel,
        out_shape=(
            jax.ShapeDtypeStruct((n // 2, k, 2 * c), BF16),
            jax.ShapeDtypeStruct((k // 2, 2 * c), BF16),
        ),
        scratch_shapes=[pltpu.VMEM((n, k, c), BF16), pltpu.VMEM((n // 8, k, c), BF16)],
        compiler_params=params(),
        name="upward",
    )(vectors, basis, child, parent)


def pairs_kernel(idx_ref, own_ref, a_ref, b_ref, blk_ref, out_ref, ext):
    step = pl.program_id(0)
    half = own_ref.shape[0]
    c = own_ref.shape[2] // 2
    slots = blk_ref.shape[1]

    @pl.when(step == 0)
    def _():
        for i, ref in enumerate((own_ref, a_ref, b_ref)):
            ext[2 * half * i : 2 * half * i + half] = ref[:, :, :c]
            ext[2 * half * i + half : 2 * half * (i + 1)] = ref[:, :, c:]
        ext[6 * half] = jnp.zeros(ext.shape[1:], BF16)

    for l in range(blk_ref.shape[0]):
        base = (step * blk_ref.shape[0] + l) * slots
        total = None
        for g in range(0, slots, 4):
            lhs = jnp.concatenate([blk_ref[l, g + j] for j in range(4)], axis=1)
            rhs = jnp.concatenate([ext[idx_ref[base + g + j]] for j in range(4)], axis=0)
            term = dot(lhs, rhs)
            total = term if total is None else total + term
        out_ref[l] = total


def pairs(idx, own, a, b, blocks, name):
    n, slots, p, q = blocks.shape
    half, k, c2 = own.shape
    whole = pl.BlockSpec((half, k, c2), lambda i, *_: (0, 0, 0))
    return pl.pallas_call(
        pairs_kernel,
        out_shape=jax.ShapeDtypeStruct((n, p, c2 // 2), F32),
        grid_spec=pltpu.PrefetchScalarGridSpec(
            num_scalar_prefetch=1,
            grid=(n // STEP,),
            in_specs=[
                whole,
                whole,
                whole,
                pl.BlockSpec((STEP, slots, p, q), lambda i, *_: (i, 0, 0, 0)),
            ],
            out_specs=pl.BlockSpec((STEP, p, c2 // 2), lambda i, *_: (i, 0, 0)),
            scratch_shapes=[pltpu.VMEM((6 * half + 1, k, c2 // 2), BF16)],
        ),
        compiler_params=params(),
        name=name,
    )(idx, own, a, b, blocks)


def join_kernel(
    s_ref, up_ref, coup_ref, par_ref, leaf_ref, near_ref, child_ref, basis_ref, send_ref, keep_ref, held, mid
):
    step = pl.program_id(0)
    core = s_ref[16]
    k = par_ref.shape[1]
    c = near_ref.shape[2]

    @pl.when(step == 0)
    def _():
        count = up_ref.shape[0]
        for i in range(count):
            held[i, : k // 2] = up_ref[i, :, :c]
            held[i, k // 2 :] = up_ref[i, :, c:]
        held[count] = jnp.zeros((k, c), BF16)
        top = None
        for g in range(0, coup_ref.shape[0], 4):
            lhs = jnp.concatenate([coup_ref[g + j] for j in range(4)], axis=1)
            rhs = jnp.concatenate([held[s_ref[g + j]] for j in range(4)], axis=0)
            term = dot(lhs, rhs)
            top = term if top is None else top + term
        top = top.astype(BF16)
        for m in range(par_ref.shape[0]):
            mid[m] = dot(par_ref[m], top).astype(BF16)

    rows = send_ref.shape[1]
    for l in range(near_ref.shape[0]):
        field = leaf_ref[l] + dot(child_ref[l], mid[step * near_ref.shape[0] // 8 + l // 8])
        part = (near_ref[l] + dot(basis_ref[l], field.astype(BF16))).astype(BF16)
        quarter = [part[rows * i : rows * (i + 1)] for i in range(4)]
        even = jnp.concatenate([quarter[0], quarter[2]], axis=1)
        odd = jnp.concatenate([quarter[1], quarter[3]], axis=1)
        keep_ref[l] = jnp.where(core == 0, even, odd)
        send_ref[l] = jnp.where(core == 0, odd, even)


def join(scalars, upper, coupling, parent, leaf_part, near_part, child, basis):
    n, p, c = near_part.shape
    k = parent.shape[1]
    full = lambda a: pl.BlockSpec(a.shape, lambda i, *_: (0,) * a.ndim)
    tile = lambda a: pl.BlockSpec((STEP,) + a.shape[1:], lambda i, *_: (i, 0, 0))
    out = jax.ShapeDtypeStruct((n, p // 4, 2 * c), BF16)
    return pl.pallas_call(
        join_kernel,
        out_shape=(out, out),
        grid_spec=pltpu.PrefetchScalarGridSpec(
            num_scalar_prefetch=1,
            grid=(n // STEP,),
            in_specs=[
                full(upper),
                full(coupling),
                full(parent),
                tile(leaf_part),
                tile(near_part),
                tile(child),
                tile(basis),
            ],
            out_specs=(tile(out), tile(out)),
            scratch_shapes=[
                pltpu.VMEM((upper.shape[0] + 1, k, c), BF16),
                pltpu.VMEM((parent.shape[0], k, c), BF16),
            ],
        ),
        compiler_params=params(),
        name="join",
    )(scalars, upper, coupling, parent, leaf_part, near_part, child, basis)


def half_kernel(s_ref, keep_ref, recv_ref, send_ref, own_ref):
    c = keep_ref.shape[2] // 2
    n = keep_ref.shape[0]
    low = s_ref[0] == 0
    total = keep_ref[...].astype(F32) + recv_ref[...].astype(F32)
    first, second = total[:, :, :c], total[:, :, c:]
    own_ref[...] = jnp.where(low, first, second)
    other = jnp.where(low, second, first).astype(BF16)
    send_ref[...] = jnp.concatenate([other[: n // 2], other[n // 2 :]], axis=-1)


def half_sum(scalars, keep, recv):
    n, rows, c2 = keep.shape
    return pl.pallas_call(
        half_kernel,
        out_shape=(
            jax.ShapeDtypeStruct((n // 2, rows, c2), BF16),
            jax.ShapeDtypeStruct((n, rows, c2 // 2), F32),
        ),
        in_specs=[pl.BlockSpec(memory_space=pltpu.SMEM), pl.BlockSpec(), pl.BlockSpec()],
        compiler_params=params(),
        name="half_sum",
    )(scalars, keep, recv)


def last_kernel(own_ref, recv_ref, out_ref):
    n = own_ref.shape[0]
    c = own_ref.shape[2]
    recv = recv_ref[...].astype(F32)
    out_ref[: n // 2] = (own_ref[: n // 2] + recv[:, :, :c]).astype(BF16)
    out_ref[n // 2 :] = (own_ref[n // 2 :] + recv[:, :, c:]).astype(BF16)


def last_sum(own, recv):
    return pl.pallas_call(
        last_kernel,
        out_shape=jax.ShapeDtypeStruct(own.shape, BF16),
        compiler_params=params(),
        name="last_sum",
    )(own, recv)


AXES = ("leaf", "rank")


def halo_pairs(leaves):
    out = []
    for leaf in range(leaves):
        for rank in range(4):
            to = leaf + 1 if rank & 1 else leaf - 1
            if 0 <= to < leaves:
                cross = 2 if {leaf, to} == {leaves // 2 - 1, leaves // 2} else 0
                out.append((leaf * 4 + rank, to * 4 + (rank ^ 1 ^ cross)))
    return out


def top_pairs(step):
    out = []
    for y_hi in range(2):
        for z in range(8):
            for x in range(4):
                for y_lo in range(2):
                    for core in range(2):
                        s = step(y_hi, z, x, y_lo, core)
                        source = (((s[0] * 8 + s[1] % 8) * 4 + s[2]) * 2 + s[3]) * 2 + s[4]
                        out.append((source, (((y_hi * 8 + z) * 4 + x) * 2 + y_lo) * 2 + core))
    return out


def collect_upper(upper):
    held = lax.ppermute(
        upper,
        AXES,
        top_pairs(lambda y_hi, z, x, y_lo, core: (y_hi ^ y_lo, z + core, x, 1 - y_lo, core)),
    )[None]
    for bit in (1, 2):
        got = lax.ppermute(
            held, AXES, top_pairs(lambda y_hi, z, x, y_lo, core: (y_hi, z, x ^ bit, y_lo, core))
        )
        held = jnp.concatenate([held, got], axis=0)
    for hop in (1, 2):
        got = lax.ppermute(
            held,
            AXES,
            top_pairs(lambda y_hi, z, x, y_lo, core: (y_hi, z + hop * (2 * core - 1), x, y_lo, core)),
        )
        held = jnp.concatenate([held, got], axis=0)
    return held


def shards(
    vectors,
    near_blocks,
    near_offsets,
    near_count,
    basis,
    child_transfer,
    parent_transfer,
    leaf_coupling,
    leaf_offsets,
    top_coupling,
    top_ids,
):
    leaf_dev, points, columns = vectors.shape
    leaves = lax.axis_size("leaf")
    total_leaves = leaf_dev * leaves
    leaf_pos = lax.axis_index("leaf")
    rank_pos = lax.axis_index("rank")
    core = rank_pos % 2
    y_lo = rank_pos // 2
    own_first = leaf_pos * leaf_dev
    ids = own_first + jnp.arange(leaf_dev, dtype=jnp.int32)
    slots = near_offsets.shape[1]

    def place(offsets):
        rel = jnp.clip(ids[:, None] + offsets, 0, total_leaves - 1) - own_first
        low = rel + jnp.where(core == 0, 2 * leaf_dev, 3 * leaf_dev)
        high = rel + jnp.where(core == 0, leaf_dev, 0)
        return jnp.where(rel < 0, low, jnp.where(rel >= leaf_dev, high, rel))

    slot_ids = rank_pos * slots + jnp.arange(slots, dtype=jnp.int32)
    near_idx = jnp.where(slot_ids[None, :] < near_count[:, None], place(near_offsets), 3 * leaf_dev)
    near_idx = near_idx.reshape(-1)
    leaf_idx = place(leaf_offsets).reshape(-1)

    route = halo_pairs(leaves)
    swap = [(i, i ^ 1) for i in range(4)]
    packed = pack(vectors)
    vec_a = lax.ppermute(packed, AXES, route)

    moments, upper = upward(vectors, basis, child_transfer, parent_transfer)
    mom_a = lax.ppermute(moments, AXES, route)

    k = parent_transfer.shape[1]
    tl = top_ids.shape[1]
    id_rows = jnp.pad(top_ids.astype(BF16), ((0, 15), (0, k - tl)))
    mixed = jnp.concatenate([top_coupling.reshape(tl * k, k), id_rows], axis=0)
    mixed = lax.all_gather(mixed, "rank", axis=0)
    coupling = mixed[:, : tl * k].reshape(4 * tl, k, k)
    all_ids = mixed[:, tl * k, :tl].reshape(-1).astype(jnp.int32)

    held = collect_upper(upper)
    y_hi, z, x = leaf_pos // 32, leaf_pos // 4 % 8, leaf_pos % 4
    turn = (2 * core - 1) * (all_ids // 4 % 8 - z - core) % 8
    here = (all_ids // 32 == (y_hi ^ y_lo)) & (turn < 4)
    position = jnp.where(here, turn * 4 + ((all_ids % 4) ^ x), 16)
    scalars = jnp.concatenate([position, core[None]]).astype(jnp.int32)

    vec_b = lax.ppermute(vec_a, "rank", swap)
    near_part = pairs(near_idx, packed, vec_a, vec_b, near_blocks, "near_pairs")
    mom_b = lax.ppermute(mom_a, "rank", swap)
    leaf_part = pairs(leaf_idx, moments, mom_a, mom_b, leaf_coupling, "leaf_pairs")

    send, keep = join(scalars, held, coupling, parent_transfer, leaf_part, near_part, child_transfer, basis)
    recv = lax.ppermute(send, "rank", swap)
    send, own = half_sum(y_lo[None].astype(jnp.int32), keep, recv)
    recv = lax.ppermute(send, "rank", [(i, i ^ 2) for i in range(4)])
    return last_sum(own, recv)


def solution(mesh):
    in_specs = (
        P("leaf", None, None),
        P("leaf", "rank", None, None),
        P("leaf", "rank"),
        P("leaf"),
        P("leaf", None, None),
        P("leaf", None, None),
        P("leaf", None, None),
        P("leaf", "rank", None, None),
        P("leaf", "rank"),
        P("leaf", "rank", None, None),
        P("leaf", "rank"),
    )
    out_specs = P("leaf", "rank", None)
    return jax.shard_map(shards, mesh=mesh, in_specs=in_specs, out_specs=out_specs, check_vma=False)
```

time: 359 us -> 77.7 us (0.22)
  blocking collectives: 226 us -> 6.49 us
  local copies, waits for them, and re-layouts: 59.2 us -> 9.68 us
  matrix products: 27.2 us -> 0 us
  Pallas kernels: 0 us -> 16.4 us
  starting transfers between devices: 12.8 us -> 28.6 us
  between operations: 13.6 us -> 0.21 us
  other arithmetic: 6.91 us -> 1.75 us
    all_gather x1, blocking collectives: 190 us -> 6.49 us  [shards(): mixed = lax.all_gather(mixed, 'rank', axis=0)]
    gather x3 -> x0, local copies, waits for them, and re-layouts: 55 us -> none  [the longest x2 33.4 us: shards(): fetched = extended[near_index]]
    psum x1 -> x0, blocking collectives: 36.2 us -> none  [shards(): lax.psum(top_part.astype(jnp.bfloat16), 'rank').astype(jnp.float32)]
    dot_general x10 -> x0, matrix products: 27.2 us -> none  [the longest x1 9.19 us: shards(): jnp.einsum('lsjk,lskr->ljr', leaf_coupling, picked, preferred_element_typ...]
    pallas_call x0 -> x7, Pallas kernels: none -> 16.4 us  [the longest x2 9.91 us: pairs(): pl.pallas_call(pairs_kernel, out_shape=jax.ShapeDtypeStruct((n, p, c2 //...]
    ppermute x4 -> x11, starting transfers between devices: 12.6 us -> 28.6 us  [the longest x1 8.1 us: collect_upper(): lax.ppermute(upper, AXES, top_pairs(lambda y_hi, z, x, y_lo, core: (y_hi...]
    ppermute x4 -> x11, waiting for transfers between devices: 0.01 us -> 13.1 us  [the longest x4 7.72 us: collect_upper(): lax.ppermute(held, AXES, top_pairs(lambda y_hi, z, x, y_lo, core: (y_hi,...]
    reduce_scatter x1 -> x0, waiting for transfers between devices: 12.3 us -> none  [shards(): lax.psum_scatter(near_part.astype(jnp.bfloat16), 'rank', scatter_dimensio...]
  transfers between devices with their start and end apart: 6 -> 11, of which waited for: 1 -> 5; matrix products, arithmetic and copies ran while one was open for 24% -> 5% of each run, Pallas kernels for 0% -> 7%
where the time goes in v1:
time: 77.7 us; the launch traced here: 76.3 us
  starting transfers between devices  28.6 us (37%)
  Pallas kernels  16.4 us (21%)
  waiting for transfers between devices  13.1 us (17%)
  local copies, waits for them, and re-layouts  9.68 us (12%)
  blocking collectives  6.49 us (8%)
  other arithmetic  1.75 us (2%)
    pallas_call x2, Pallas kernels, pairs(): pl.pallas_call(pairs_kernel, out_shape=jax.ShapeDtypeStruct((n, p, c2 //...  9.91 us
    unnamed x23, local copies, waits for them, and re-layouts  8.11 us
    ppermute x1, starting transfers between devices, collect_upper(): lax.ppermute(upper, AXES, top_pairs(lambda y_hi, z, x, y_lo, core: (y_hi...  8.1 us
    ppermute x4, waiting for transfers between devices, collect_upper(): lax.ppermute(held, AXES, top_pairs(lambda y_hi, z, x, y_lo, core: (y_hi,...  7.72 us
    all_gather x1, blocking collectives, shards(): mixed = lax.all_gather(mixed, 'rank', axis=0)  6.49 us
    ppermute x4, starting transfers between devices, collect_upper(): lax.ppermute(held, AXES, top_pairs(lambda y_hi, z, x, y_lo, core: (y_hi,...  6.36 us
    ppermute x1, starting transfers between devices, shards(): recv = lax.ppermute(send, 'rank', swap)  5.75 us
    ppermute x1, starting transfers between devices, shards(): mom_a = lax.ppermute(moments, AXES, route)  4.5 us
  transfers between devices with their start and end apart: 11, of which 5 were waited for; matrix products, arithmetic and copies ran while one was open for 5% of the time, Pallas kernels for 7%

profile of v1, /device:TPU:1, one launch (start us, length us, event | category | flops | bytes accessed | tf_op | source)
XLA Modules:
  0.0 76.3 jit_solution(18266818105038634344)
XLA Ops:
  0.0 1.2 %copy-done.2 = bf16[64,64,64]{2,1,0:T(8,128)(2,1)S(1)} copy-done((bf16[64,64,64]{2,1,0:T(8,128)(2,1)S(1)}, bf16[64,64,64]{2,1,0:T(8,128)(2,1)}, u32[]{:S(2)}) %copy-start.2) | copy-done | bytes 524312
  1.2 1.2 %copy-done.3 = bf16[64,64,64]{2,1,0:T(8,128)(2,1)S(1)} copy-done((bf16[64,64,64]{2,1,0:T(8,128)(2,1)S(1)}, bf16[64,64,64]{2,1,0:T(8,128)(2,1)}, u32[]{:S(2)}) %copy-start.3) | copy-done | bytes 524312
  2.5 1.2 %copy-done.5 = bf16[64,64,64]{2,1,0:T(8,128)(2,1)S(1)} copy-done((bf16[64,64,64]{2,1,0:T(8,128)(2,1)S(1)}, bf16[64,64,64]{2,1,0:T(8,128)(2,1)}, u32[]{:S(2)}) %copy-start.5) | copy-done | bytes 524312
  3.7 0.9 %copy-done.7 = bf16[8,64,64]{2,1,0:T(8,128)(2,1)S(1)} copy-done((bf16[8,64,64]{2,1,0:T(8,128)(2,1)S(1)}, bf16[8,64,64]{2,1,0:T(8,128)(2,1)}, u32[]{:S(2)}) %copy-start.7) | copy-done | bytes 65560
  4.6 1.1 %upward.1 = (bf16[32,64,128]{2,1,0:T(8,128)(2,1)S(1)}, bf16[32,128]{1,0:T(8,128)(2,1)S(1)}) custom-call(bf16[64,64,64]{2,1,0:T(8,128)(2,1)S(1)} %copy-done.2, bf16[64,64,64]{2,1,0:T(8,128)(2,1)S(1)} %copy-done.3, bf16[64,64,64]{2,1,0:T(8,128)(2,1)S(1)} %copy-done.5, bf16[8,64,64]{2,1,0:T(8,128)(2,1)S(1)} %copy-done.7), custom_call_target="tpu_custom_call" | custom-call | tf_op jit(solution)/shard_map/upward/pallas_call | solution.py:59
  5.6 4.5 %collective-permute-start.5 = (bf16[32,64,128]{2,1,0:T(8,128)(2,1)S(1)}, bf16[32,64,128]{2,1,0:T(8,128)(2,1)S(1)}, u32[]{:S(2)}, u32[]{:S(2)}) collective-permute-start(bf16[32,64,128]{2,1,0:T(8,128)(2,1)S(1)} %get-tuple-element.12.own_ref), channel_id=1, source_target_pairs={{1,4},{3,6},{4,1},{5,8},{6,3},{7,10},{8,5},{9,12},{10,7},{11,14},{... | collective-permute-start | bytes 1572872 | tf_op jit(solution)/shard_map/ppermute | solution.py:318
  10.1 0.2 pack_vectors.1.own_ref
  10.4 1.9 %collective-permute-start.7 = (bf16[32,64,128]{2,1,0:T(8,128)(2,1)S(1)}, bf16[32,64,128]{2,1,0:T(8,128)(2,1)S(1)}, u32[]{:S(2)}, u32[]{:S(2)}) collective-permute-start(bf16[32,64,128]{2,1,0:T(8,128)(2,1)S(1)} %pack_vectors.1.own_ref), channel_id=1, source_target_pairs={{1,4},{3,6},{4,1},{5,8},{6,3},{7,10},{8,5},{9,12},{10,7},{11,14},{... | collective-permute-start | bytes 1572872 | tf_op jit(solution)/shard_map/ppermute | solution.py:315
  12.3 8.1 %collective-permute-start = (bf16[32,128]{1,0:T(8,128)(2,1)S(1)}, bf16[32,128]{1,0:T(8,128)(2,1)S(1)}, u32[]{:S(2)}, u32[]{:S(2)}) collective-permute-start(bf16[32,128]{1,0:T(8,128)(2,1)S(1)} %get-tuple-element.11), channel_id=1, source_target_pairs={{2,0},{19,1},{128,2},{145,3},{6,4},{23,5},{132,6},{149,7},{10,8},{... | collective-permute-start | bytes 24584 | tf_op jit(solution)/shard_map/ppermute | solution.py:257
  20.4 0.9 %copy.33 = bf16[256,64]{0,1:T(8,128)(2,1)S(1)} copy(bf16[256,64]{1,0:T(8,128)(2,1)} %bitcast.13) | data formatting | bytes 65536 | tf_op jit(solution)/shard_map/reshape | solution.py:323
  21.3 0.7 convert_element_type.11
  22.1 6.5 %all-gather.1 = bf16[4,272,64]{1,2,0:T(8,128)(2,1)S(1)} all-gather(bf16[1,272,64]{1,2,0:T(8,128)(2,1)S(1)} %fusion.2), channel_id=2, replica_groups=mesh['leaf'=64,'rank'=4] {'rank'}, dimensions={0}, use_global_device_ids=true | all-gather | bytes 174080 | tf_op jit(solution)/shard_map/all_gather | solution.py:324
  28.6 0.1 convert_reduce_fusion
  28.9 0.8 %fusion.5 = (s32[64,8]{0,1:T(8,128)S(1)}, s32[64,8]{0,1:T(8,128)S(1)}) fusion(s32[64,8]{0,1:T(8,128)} %param.13, s32[64]{0:T(128)} %param.14, s32[]{:T(128)S(6)} %select_n.90, s32[]{:T(128)S(6)} %select_n.89, s32[]{:T(128)S(6)} %mul.22, s32[64]{0:T(128)S(1)} %iota_add_fusion.1, s32[8]{0:T(128)S(1)} %iota_add_fusion, s32[64,8]{0,1:T(8,128)} %param.19), kind=kLoop, calls=%fused_computation.17 | loop fusion | flops 10240 | bytes 8748 | tf_op jit(solution)/shard_map/jit(_where)/select_n | solution.py:308
  30.1 0.2 copy.30
  30.4 2.5 %collective-permute-done.1 = bf16[1,32,128]{2,1,0:T(8,128)(2,1)S(1)} collective-permute-done((bf16[1,32,128]{2,1,0:T(8,128)(2,1)S(1)}, bf16[1,32,128]{2,1,0:T(8,128)(2,1)S(1)}, u32[]{:S(2)}, u32[]{:S(2)}) %collective-permute-start.1) | collective-permute-done | bytes 8224 | tf_op jit(solution)/shard_map/ppermute | solution.py:263
  32.9 4.0 %collective-permute-start.2 = (bf16[2,32,128]{2,1,0:T(8,128)(2,1)S(1)}, bf16[2,32,128]{2,1,0:T(8,128)(2,1)S(1)}, u32[]{:S(2)}, u32[]{:S(2)}) collective-permute-start(bf16[2,32,128]{2,1,0:T(8,128)(2,1)S(1)} %pad_maximum_fusion.2), channel_id=1, source_target_pairs={{8,0},{9,1},{10,2},{11,3},{12,4},{13,5},{14,6},{15,7},{0,8},{1,9},... | collective-permute-start | bytes 49160 | tf_op jit(solution)/shard_map/ppermute | solution.py:263
  36.9 1.3 %collective-permute-start.6 = (bf16[32,64,128]{2,1,0:T(8,128)(2,1)S(1)}, bf16[32,64,128]{2,1,0:T(8,128)(2,1)S(1)}, u32[]{:S(2)}, u32[]{:S(2)}) collective-permute-start(bf16[32,64,128]{2,1,0:T(8,128)(2,1)S(1)} %collective-permute-done.5.a_ref), channel_id=1, source_target_pairs={{0,1},{1,0},{2,3},{3,2},{4,5},{5,4},{6,7},{7,6},{8,9},{9,8},{10,11... | collective-permute-start | bytes 1572872 | tf_op jit(solution)/shard_map/ppermute | solution.py:337
  38.4 0.9 %collective-permute-start.3 = (bf16[4,32,128]{2,1,0:T(8,128)(2,1)S(1)}, bf16[4,32,128]{2,1,0:T(8,128)(2,1)S(1)}, u32[]{:S(2)}, u32[]{:S(2)}) collective-permute-start(bf16[4,32,128]{2,1,0:T(8,128)(2,1)S(1)} %pad_maximum_fusion.1), channel_id=1, source_target_pairs={{112,0},{17,1},{114,2},{19,3},{116,4},{21,5},{118,6},{23,7},{120,8... | collective-permute-start | bytes 98312 | tf_op jit(solution)/shard_map/ppermute | solution.py:268
  39.3 1.9 %collective-permute-done.3 = bf16[4,32,128]{2,1,0:T(8,128)(2,1)S(1)} collective-permute-done((bf16[4,32,128]{2,1,0:T(8,128)(2,1)S(1)}, bf16[4,32,128]{2,1,0:T(8,128)(2,1)S(1)}, u32[]{:S(2)}, u32[]{:S(2)}) %collective-permute-start.3) | collective-permute-done | bytes 32800 | tf_op jit(solution)/shard_map/ppermute | solution.py:268
  41.2 1.4 %collective-permute-start.4 = (bf16[8,32,128]{2,1,0:T(8,128)(2,1)S(1)}, bf16[8,32,128]{2,1,0:T(8,128)(2,1)S(1)}, u32[]{:S(2)}, u32[]{:S(2)}) collective-permute-start(bf16[8,32,128]{2,1,0:T(8,128)(2,1)S(1)} %pad_maximum_fusion), channel_id=1, source_target_pairs={{96,0},{33,1},{98,2},{35,3},{100,4},{37,5},{102,6},{39,7},{104,8},... | collective-permute-start | bytes 196616 | tf_op jit(solution)/shard_map/ppermute | solution.py:268
  42.6 3.3 %collective-permute-done.4 = bf16[8,32,128]{2,1,0:T(8,128)(2,1)S(1)} collective-permute-done((bf16[8,32,128]{2,1,0:T(8,128)(2,1)S(1)}, bf16[8,32,128]{2,1,0:T(8,128)(2,1)S(1)}, u32[]{:S(2)}, u32[]{:S(2)}) %collective-permute-start.4) | collective-permute-done | bytes 65568 | tf_op jit(solution)/shard_map/ppermute | solution.py:268
  45.9 3.4 %copy-done = bf16[64,8,64,64]{3,2,1,0:T(8,128)(2,1)S(1)} copy-done((bf16[64,8,64,64]{3,2,1,0:T(8,128)(2,1)S(1)}, bf16[64,8,64,64]{3,2,1,0:T(8,128)(2,1)}, u32[]{:S(2)}) %copy-start) | copy-done | bytes 4194328
  49.3 5.0 %leaf_pairs.1.leaf_ref = f32[64,64,64]{2,1,0:T(8,128)S(1)} custom-call(s32[512]{0:T(512)S(1)} %reshape.25.idx_ref, bf16[32,64,128]{2,1,0:T(8,128)(2,1)S(1)} %get-tuple-element.12.own_ref, bf16[32,64,128]{2,1,0:T(8,128)(2,1)S(1)} %collective-permute-done.5.a_ref, bf16[32,64,128]{2,1,0:T(8,128)(2,1)S(1)} %collective-permute-done.6.b_ref, ...), custom_call_target="tpu_custom_call" | custom-call | tf_op jit(solution)/shard_map/leaf_pairs/pallas_call | solution.py:99
  54.3 5.0 %near_pairs.1.near_ref = f32[64,64,64]{2,1,0:T(8,128)S(1)} custom-call(s32[512]{0:T(512)S(1)} %reshape.26.idx_ref, bf16[32,64,128]{2,1,0:T(8,128)(2,1)S(1)} %pack_vectors.1.own_ref, bf16[32,64,128]{2,1,0:T(8,128)(2,1)S(1)} %collective-permute-done.7.a_ref, bf16[32,64,128]{2,1,0:T(8,128)(2,1)S(1)} %collective-permute-done.8.b_ref, ...), custom_call_target="tpu_custom_call" | custom-call | tf_op jit(solution)/shard_map/near_pairs/pallas_call | solution.py:99
  59.3 4.2 %join.1 = (bf16[64,16,128]{2,1,0:T(8,128)(2,1)S(1)}, bf16[64,16,128]{2,1,0:T(8,128)(2,1)S(1)}) custom-call(s32[17]{0:T(128)S(1)} %pad_add_fusion.s_ref, bf16[16,32,128]{2,1,0:T(8,128)(2,1)S(1)} %constant_dynamic-update-slice_fusion.up_ref, bf16[16,64,64]{2,1,0:T(8,128)(2,1)S(1)} %bitcast.8, bf16[8,64,64]{2,1,0:T(8,128)(2,1)S(1)} %copy-done.8, ...), custom_call_target="tpu_custom_call" | custom-call | tf_op jit(solution)/shard_map/join/pallas_call | solution.py:161
  63.5 5.7 %collective-permute-start.9 = (bf16[64,16,128]{2,1,0:T(8,128)(2,1)S(1)}, bf16[64,16,128]{2,1,0:T(8,128)(2,1)S(1)}, u32[]{:S(2)}, u32[]{:S(2)}) collective-permute-start(bf16[64,16,128]{2,1,0:T(8,128)(2,1)S(1)} %get-tuple-element.14), channel_id=1, source_target_pairs={{0,1},{1,0},{2,3},{3,2},{4,5},{5,4},{6,7},{7,6},{8,9},{9,8},{10,11... | collective-permute-start | bytes 786440 | tf_op jit(solution)/shard_map/ppermute | solution.py:341
  69.3 1.2 %collective-permute-done.9.recv_ref = bf16[64,16,128]{2,1,0:T(8,128)(2,1)S(1)} collective-permute-done((bf16[64,16,128]{2,1,0:T(8,128)(2,1)S(1)}, bf16[64,16,128]{2,1,0:T(8,128)(2,1)S(1)}, u32[]{:S(2)}, u32[]{:S(2)}) %collective-permute-start.9) | collective-permute-done | bytes 262176 | tf_op jit(solution)/shard_map/ppermute | solution.py:341
  70.4 0.2 half_sum.1
  70.7 0.5 collective-permute-start.10
  71.2 4.3 %collective-permute-done.10.recv_ref = bf16[32,16,128]{2,1,0:T(8,128)(2,1)S(1)} collective-permute-done((bf16[32,16,128]{2,1,0:T(8,128)(2,1)S(1)}, bf16[32,16,128]{2,1,0:T(8,128)(2,1)S(1)}, u32[]{:S(2)}, u32[]{:S(2)}) %collective-permute-start.10) | collective-permute-done | bytes 131104 | tf_op jit(solution)/shard_map/ppermute | solution.py:343
  75.5 0.8 %last_sum.1 = bf16[64,16,64]{2,1,0:T(8,128)(2,1)} custom-call(f32[64,16,64]{2,1,0:T(8,128)S(1)} %get-tuple-element.15.own_ref, bf16[32,16,128]{2,1,0:T(8,128)(2,1)S(1)} %collective-permute-done.10.recv_ref), custom_call_target="tpu_custom_call" | custom-call | tf_op jit(solution)/shard_map/last_sum/pallas_call | solution.py:221
  (41 shorter events, 1.0 us)
Async XLA Ops:
  0.0 1.2 %copy-start.2 = (bf16[64,64,64]{2,1,0:T(8,128)(2,1)S(1)}, bf16[64,64,64]{2,1,0:T(8,128)(2,1)}, u32[]{:S(2)}) copy-start(bf16[64,64,64]{2,1,0:T(8,128)(2,1)} %v_ref.3) | copy-start | bytes 1572868
  1.2 1.2 %copy-start.3 = (bf16[64,64,64]{2,1,0:T(8,128)(2,1)S(1)}, bf16[64,64,64]{2,1,0:T(8,128)(2,1)}, u32[]{:S(2)}) copy-start(bf16[64,64,64]{2,1,0:T(8,128)(2,1)} %basis_ref.1) | copy-start | bytes 1572868
  2.5 1.2 %copy-start.5 = (bf16[64,64,64]{2,1,0:T(8,128)(2,1)S(1)}, bf16[64,64,64]{2,1,0:T(8,128)(2,1)}, u32[]{:S(2)}) copy-start(bf16[64,64,64]{2,1,0:T(8,128)(2,1)} %child_ref.1) | copy-start | bytes 1572868
  3.7 0.9 %copy-start.7 = (bf16[8,64,64]{2,1,0:T(8,128)(2,1)S(1)}, bf16[8,64,64]{2,1,0:T(8,128)(2,1)}, u32[]{:S(2)}) copy-start(bf16[8,64,64]{2,1,0:T(8,128)(2,1)} %par_ref.1) | copy-start | bytes 196612
  5.6 31.3 %collective-permute-start.5 = (bf16[32,64,128]{2,1,0:T(8,128)(2,1)S(1)}, bf16[32,64,128]{2,1,0:T(8,128)(2,1)S(1)}, u32[]{:S(2)}, u32[]{:S(2)}) collective-permute-start(bf16[32,64,128]{2,1,0:T(8,128)(2,1)S(1)} %get-tuple-element.12.own_ref), channel_id=1, source_target_pairs={{1,4},{3,6},{4,1},{5,8},{6,3},{7,10},{8,5},{9,12},{10,7},{11,14},{... | collective-permute-start | bytes 1572872 | tf_op jit(solution)/shard_map/ppermute | solution.py:318
  10.4 27.9 %collective-permute-start.7 = (bf16[32,64,128]{2,1,0:T(8,128)(2,1)S(1)}, bf16[32,64,128]{2,1,0:T(8,128)(2,1)S(1)}, u32[]{:S(2)}, u32[]{:S(2)}) collective-permute-start(bf16[32,64,128]{2,1,0:T(8,128)(2,1)S(1)} %pack_vectors.1.own_ref), channel_id=1, source_target_pairs={{1,4},{3,6},{4,1},{5,8},{6,3},{7,10},{8,5},{9,12},{10,7},{11,14},{... | collective-permute-start | bytes 1572872 | tf_op jit(solution)/shard_map/ppermute | solution.py:315
  12.3 18.0 %collective-permute-start = (bf16[32,128]{1,0:T(8,128)(2,1)S(1)}, bf16[32,128]{1,0:T(8,128)(2,1)S(1)}, u32[]{:S(2)}, u32[]{:S(2)}) collective-permute-start(bf16[32,128]{1,0:T(8,128)(2,1)S(1)} %get-tuple-element.11), channel_id=1, source_target_pairs={{2,0},{19,1},{128,2},{145,3},{6,4},{23,5},{132,6},{149,7},{10,8},{... | collective-permute-start | bytes 24584 | tf_op jit(solution)/shard_map/ppermute | solution.py:257
  30.3 2.6 %collective-permute-start.1 = (bf16[1,32,128]{2,1,0:T(8,128)(2,1)S(1)}, bf16[1,32,128]{2,1,0:T(8,128)(2,1)S(1)}, u32[]{:S(2)}, u32[]{:S(2)}) collective-permute-start(bf16[1,32,128]{2,1,0:T(8,128)(2,1)S(1)} %bitcast.9), channel_id=1, source_target_pairs={{4,0},{5,1},{6,2},{7,3},{0,4},{1,5},{2,6},{3,7},{12,8},{13,9},{14,... | collective-permute-start | bytes 24584 | tf_op jit(solution)/shard_map/ppermute | solution.py:263
  32.9 5.4 %collective-permute-start.2 = (bf16[2,32,128]{2,1,0:T(8,128)(2,1)S(1)}, bf16[2,32,128]{2,1,0:T(8,128)(2,1)S(1)}, u32[]{:S(2)}, u32[]{:S(2)}) collective-permute-start(bf16[2,32,128]{2,1,0:T(8,128)(2,1)S(1)} %pad_maximum_fusion.2), channel_id=1, source_target_pairs={{8,0},{9,1},{10,2},{11,3},{12,4},{13,5},{14,6},{15,7},{0,8},{1,9},... | collective-permute-start | bytes 49160 | tf_op jit(solution)/shard_map/ppermute | solution.py:263
  36.9 9.0 %collective-permute-start.6 = (bf16[32,64,128]{2,1,0:T(8,128)(2,1)S(1)}, bf16[32,64,128]{2,1,0:T(8,128)(2,1)S(1)}, u32[]{:S(2)}, u32[]{:S(2)}) collective-permute-start(bf16[32,64,128]{2,1,0:T(8,128)(2,1)S(1)} %collective-permute-done.5.a_ref), channel_id=1, source_target_pairs={{0,1},{1,0},{2,3},{3,2},{4,5},{5,4},{6,7},{7,6},{8,9},{9,8},{10,11... | collective-permute-start | bytes 1572872 | tf_op jit(solution)/shard_map/ppermute | solution.py:337
  38.2 16.1 %collective-permute-start.8 = (bf16[32,64,128]{2,1,0:T(8,128)(2,1)S(1)}, bf16[32,64,128]{2,1,0:T(8,128)(2,1)S(1)}, u32[]{:S(2)}, u32[]{:S(2)}) collective-permute-start(bf16[32,64,128]{2,1,0:T(8,128)(2,1)S(1)} %collective-permute-done.7.a_ref), channel_id=1, source_target_pairs={{0,1},{1,0},{2,3},{3,2},{4,5},{5,4},{6,7},{7,6},{8,9},{9,8},{10,11... | collective-permute-start | bytes 1572872 | tf_op jit(solution)/shard_map/ppermute | solution.py:335
  38.4 2.8 %collective-permute-start.3 = (bf16[4,32,128]{2,1,0:T(8,128)(2,1)S(1)}, bf16[4,32,128]{2,1,0:T(8,128)(2,1)S(1)}, u32[]{:S(2)}, u32[]{:S(2)}) collective-permute-start(bf16[4,32,128]{2,1,0:T(8,128)(2,1)S(1)} %pad_maximum_fusion.1), channel_id=1, source_target_pairs={{112,0},{17,1},{114,2},{19,3},{116,4},{21,5},{118,6},{23,7},{120,8... | collective-permute-start | bytes 98312 | tf_op jit(solution)/shard_map/ppermute | solution.py:268
  41.2 4.7 %collective-permute-start.4 = (bf16[8,32,128]{2,1,0:T(8,128)(2,1)S(1)}, bf16[8,32,128]{2,1,0:T(8,128)(2,1)S(1)}, u32[]{:S(2)}, u32[]{:S(2)}) collective-permute-start(bf16[8,32,128]{2,1,0:T(8,128)(2,1)S(1)} %pad_maximum_fusion), channel_id=1, source_target_pairs={{96,0},{33,1},{98,2},{35,3},{100,4},{37,5},{102,6},{39,7},{104,8},... | collective-permute-start | bytes 196616 | tf_op jit(solution)/shard_map/ppermute | solution.py:268
  45.9 3.4 %copy-start = (bf16[64,8,64,64]{3,2,1,0:T(8,128)(2,1)S(1)}, bf16[64,8,64,64]{3,2,1,0:T(8,128)(2,1)}, u32[]{:S(2)}) copy-start(bf16[64,8,64,64]{3,2,1,0:T(8,128)(2,1)} %blk_ref.2) | copy-start | bytes 12582916
  49.3 5.0 %copy-start.1 = (bf16[64,8,64,64]{3,2,1,0:T(8,128)(2,1)S(1)}, bf16[64,8,64,64]{3,2,1,0:T(8,128)(2,1)}, u32[]{:S(2)}) copy-start(bf16[64,8,64,64]{3,2,1,0:T(8,128)(2,1)} %blk_ref.3) | copy-start | bytes 12582916
  54.3 5.0 %copy-start.4 = (bf16[64,64,64]{2,1,0:T(8,128)(2,1)S(1)}, bf16[64,64,64]{2,1,0:T(8,128)(2,1)}, u32[]{:S(2)}) copy-start(bf16[64,64,64]{2,1,0:T(8,128)(2,1)} %basis_ref.1) | copy-start | bytes 1572868
  54.3 5.0 %copy-start.6 = (bf16[64,64,64]{2,1,0:T(8,128)(2,1)S(1)}, bf16[64,64,64]{2,1,0:T(8,128)(2,1)}, u32[]{:S(2)}) copy-start(bf16[64,64,64]{2,1,0:T(8,128)(2,1)} %child_ref.1) | copy-start | bytes 1572868
  54.3 5.0 %copy-start.8 = (bf16[8,64,64]{2,1,0:T(8,128)(2,1)S(1)}, bf16[8,64,64]{2,1,0:T(8,128)(2,1)}, u32[]{:S(2)}) copy-start(bf16[8,64,64]{2,1,0:T(8,128)(2,1)} %par_ref.1) | copy-start | bytes 196612
  63.5 6.9 %collective-permute-start.9 = (bf16[64,16,128]{2,1,0:T(8,128)(2,1)S(1)}, bf16[64,16,128]{2,1,0:T(8,128)(2,1)S(1)}, u32[]{:S(2)}, u32[]{:S(2)}) collective-permute-start(bf16[64,16,128]{2,1,0:T(8,128)(2,1)S(1)} %get-tuple-element.14), channel_id=1, source_target_pairs={{0,1},{1,0},{2,3},{3,2},{4,5},{5,4},{6,7},{7,6},{8,9},{9,8},{10,11... | collective-permute-start | bytes 786440 | tf_op jit(solution)/shard_map/ppermute | solution.py:341
  70.7 4.8 %collective-permute-start.10 = (bf16[32,16,128]{2,1,0:T(8,128)(2,1)S(1)}, bf16[32,16,128]{2,1,0:T(8,128)(2,1)S(1)}, u32[]{:S(2)}, u32[]{:S(2)}) collective-permute-start(bf16[32,16,128]{2,1,0:T(8,128)(2,1)S(1)} %get-tuple-element.16), channel_id=1, source_target_pairs={{0,2},{1,3},{2,0},{3,1},{4,6},{5,7},{6,4},{7,5},{8,10},{9,11},{10,... | collective-permute-start | bytes 393224 | tf_op jit(solution)/shard_map/ppermute | solution.py:343

commit v2 on v0

v2 whole, which is shorter than its diff:
```python
import functools

import jax
import jax.numpy as jnp
from jax import lax
from jax.experimental import pallas as pl
from jax.experimental.pallas import tpu as pltpu
from jax.sharding import PartitionSpec as P

F32 = jnp.float32
BF16 = jnp.bfloat16
MIB = 1024 * 1024
VMEM = pl.BlockSpec(memory_space=pltpu.VMEM)
SMEM = pl.BlockSpec(memory_space=pltpu.SMEM)


def params(mib):
    return pltpu.CompilerParams(vmem_limit_bytes=mib * MIB)


def cost(us):
    return pl.CostEstimate(flops=0, bytes_accessed=int(us * 3.0e6), transcendentals=0)


def dot(a, b):
    return jnp.dot(a, b, preferred_element_type=F32)


def dot_t(a, b):
    return lax.dot_general(a, b, (((0,), (0,)), ((), ())), preferred_element_type=F32)


def pinned(*arrays):
    return [pltpu.with_memory_space_constraint(a, pltpu.HBM) for a in arrays]


def load(sources, targets, sems):
    copies = [pltpu.make_async_copy(a, b, sems.at[i]) for i, (a, b) in enumerate(zip(sources, targets))]
    for copy in copies:
        copy.start()
    return copies


def left_right(left, right):
    lane = lax.broadcasted_iota(jnp.int32, left.shape, left.ndim - 1)
    return jnp.where(lane < left.shape[-1] // 2, left, right)


def first_kernel(
    pos_ref, v_any, b_any, c_any, p_any, t_any, ids_any, near_any, count_any, leaf_any,
    out_ref, coup_ref, up_ref, near_idx, leaf_idx,
    v, b, c, p, t, ids, near, count, leaf, mid, sems, *, total,
):
    copies = load(
        (v_any, b_any, c_any, p_any, near_any, count_any, leaf_any, t_any, ids_any),
        (v, b, c, p, near, count, leaf, t, ids),
        sems,
    )
    n, _, k = b.shape
    cols = v.shape[2]
    half = n // 2
    copies[0].wait()
    out_ref[:half] = jnp.concatenate([v[:half], v[half:]], axis=-1)
    copies[1].wait()
    for i in range(half):
        both = dot_t(jnp.concatenate([b[i], b[half + i]], axis=1), out_ref[i])
        out_ref[half + i] = left_right(both[:k], both[k:]).astype(BF16)
    copies[2].wait()
    for m in range(n // 16):
        here = out_ref[half + 8 * m : half + 8 * m + 8].reshape(8 * k, 2 * cols)
        low = dot_t(c[8 * m : 8 * m + 8].reshape(8 * k, k), here)
        high = dot_t(c[half + 8 * m : half + 8 * m + 8].reshape(8 * k, k), here)
        mid[m] = left_right(low, high).astype(BF16)
    copies[3].wait()
    mids = n // 16
    here = mid[...].reshape(mids * k, 2 * cols)
    low = dot_t(p[:mids].reshape(mids * k, k), here)
    high = dot_t(p[mids:].reshape(mids * k, k), here)
    up = (low[:, :cols] + high[:, cols:]).astype(BF16)
    up_ref[...] = jnp.concatenate([up[: k // 2], up[k // 2 :]], axis=-1)

    slots = near.shape[0]
    own_first = pos_ref[0] * n
    rank = pos_ref[1]
    side = pos_ref[2]
    leaf_ids = own_first + lax.broadcasted_iota(jnp.int32, near.shape, 1)

    def place(offsets):
        rel = jnp.clip(leaf_ids + offsets, 0, total - 1) - own_first
        under = rel + jnp.where(side == 0, 2 * n, 3 * n)
        over = rel + jnp.where(side == 0, n, 0)
        return jnp.where(rel < 0, under, jnp.where(rel >= n, over, rel))

    slot = rank * slots + lax.broadcasted_iota(jnp.int32, near.shape, 0)
    for copy in copies[4:]:
        copy.wait()
    near_idx[...] = jnp.where(slot < count[...], place(near[...]), 3 * n)
    leaf_idx[...] = place(leaf[...])

    top_slots = t.shape[0] // 2
    coup_ref[:top_slots] = jnp.concatenate([t[:top_slots], t[top_slots:]], axis=-1)
    lane = lax.broadcasted_iota(jnp.int32, coup_ref.shape[1:], 1)
    row = jnp.zeros(coup_ref.shape[1:], F32)
    for s in range(2 * top_slots):
        row = jnp.where(lane == s, ids[0, s].astype(F32), row)
    coup_ref[top_slots] = row.astype(BF16)


def first(pos, ids, vectors, coupling, basis, child, parent, near_offsets, near_count, leaf_offsets, total):
    n, p, c = vectors.shape
    k = basis.shape[2]
    sources = (vectors, basis, child, parent, coupling)
    small = (ids, near_offsets, near_count, leaf_offsets)
    shape = near_offsets.shape
    return pl.pallas_call(
        functools.partial(first_kernel, total=total),
        out_shape=(
            jax.ShapeDtypeStruct((n, p, 2 * c), BF16),
            jax.ShapeDtypeStruct((coupling.shape[0] // 2 + 1, k, 2 * k), BF16),
            jax.ShapeDtypeStruct((k // 2, 2 * c), BF16),
            jax.ShapeDtypeStruct(shape, jnp.int32),
            jax.ShapeDtypeStruct(shape, jnp.int32),
        ),
        in_specs=[SMEM] + [pl.BlockSpec(memory_space=pltpu.HBM)] * 9,
        out_specs=(VMEM,) * 5,
        scratch_shapes=[pltpu.VMEM(a.shape, BF16) for a in sources]
        + [
            pltpu.SMEM(ids.shape, jnp.int32),
            pltpu.VMEM(shape, jnp.int32),
            pltpu.VMEM(near_count.shape, jnp.int32),
            pltpu.VMEM(shape, jnp.int32),
            pltpu.VMEM((n // 16, k, 2 * c), BF16),
            pltpu.SemaphoreType.DMA((9,)),
        ],
        compiler_params=params(16),
        cost_estimate=cost(3.0),
        name="first",
    )(pos, *pinned(*sources, *small))


CHUNK = 8
AHEAD = 3


def fields_kernel(
    near_idx, leaf_idx, own_ref, a_ref, b_ref, near_any, leaf_any, near_out, leaf_out, near, leaf, vec, mom, sems
):
    n, slots, p, k = near.shape
    chunks = n // CHUNK
    parts = []
    for i in range(chunks):
        rows = pl.ds(i * CHUNK, CHUNK)
        parts.append(
            [
                pltpu.make_async_copy(src.at[rows], dst.at[rows], sems.at[2 * i + j])
                for j, (src, dst) in enumerate(((near_any, near), (leaf_any, leaf)))
            ]
        )
    for i in range(AHEAD):
        for c in parts[i]:
            c.start()
    half = n // 2
    cols = own_ref.shape[2] // 2
    for i, ref in enumerate((own_ref, a_ref, b_ref)):
        for to, first in ((vec, 0), (mom, half)):
            to[n * i : n * i + half] = ref[first : first + half, :, :cols]
            to[n * i + half : n * (i + 1)] = ref[first : first + half, :, cols:]
    vec[3 * n] = jnp.zeros(vec.shape[1:], BF16)

    for i in range(chunks):
        for c in parts[i]:
            c.wait()
        if i + AHEAD < chunks:
            for c in parts[i + AHEAD]:
                c.start()
        for blocks, idx, store, out in ((near, near_idx, vec, near_out), (leaf, leaf_idx, mom, leaf_out)):
            for l in range(i * CHUNK, (i + 1) * CHUNK):
                total = None
                for g in range(0, slots, 4):
                    lhs = jnp.concatenate([blocks[l, g + j] for j in range(4)], axis=1)
                    rhs = jnp.concatenate([store[idx[g + j, l]] for j in range(4)], axis=0)
                    term = dot(lhs, rhs)
                    total = term if total is None else total + term
                out[l] = total


def fields(near_idx, leaf_idx, own, a, b, near, leaf):
    n, slots, p, k = near.shape
    c = own.shape[2] // 2
    out = jax.ShapeDtypeStruct((n, p, c), F32)
    return pl.pallas_call(
        fields_kernel,
        out_shape=(out, out),
        in_specs=[SMEM] * 2 + [VMEM] * 3 + [pl.BlockSpec(memory_space=pltpu.HBM)] * 2,
        out_specs=(VMEM, VMEM),
        scratch_shapes=[
            pltpu.VMEM(near.shape, BF16),
            pltpu.VMEM(leaf.shape, BF16),
            pltpu.VMEM((3 * n + 1, p, c), BF16),
            pltpu.VMEM((3 * n, k, c), BF16),
            pltpu.SemaphoreType.DMA((2 * n // CHUNK,)),
        ],
        compiler_params=params(26),
        cost_estimate=cost(8.0),
        name="fields",
    )(near_idx, leaf_idx, own, a, b, *pinned(near, leaf))


def join_kernel(
    pos_ref, up_ref, other_ref, coup0_ref, coup1_ref, coup2_ref, coup3_ref, par_ref, leaf_ref, near_ref, child_ref, basis_ref,
    send_ref, keep_ref, held, mid, where_v, where_s, sem,
):
    k = par_ref.shape[1]
    cols = near_ref.shape[2]
    half = up_ref.shape[0]
    count = 2 * half
    leaf_pos, rank = pos_ref[0], pos_ref[1]
    core = rank & 1
    blocks = (coup0_ref, coup1_ref, coup2_ref, coup3_ref)
    slots = coup0_ref.shape[0] - 1
    for r, block in enumerate(blocks):
        ids = block[slots, :16].astype(F32).astype(jnp.int32)[:8]
        dz = ((ids >> 2) & 7) ^ ((leaf_pos >> 2) & 7) ^ (4 * core)
        dx = (ids & 3) ^ (leaf_pos & 3)
        here = ((ids >> 5) == ((leaf_pos >> 5) ^ (rank >> 1))) & (dz < 4)
        where_v[r] = jnp.where(here, (dz & 1) + 2 * dx + 8 * (dz >> 1), count)
    copy = pltpu.make_async_copy(where_v, where_s, sem)
    copy.start()
    for start, ref in ((0, up_ref), (half, other_ref)):
        for i in range(half):
            held[start + i, : k // 2] = ref[i, :, :cols]
            held[start + i, k // 2 :] = ref[i, :, cols:]
    held[count] = jnp.zeros((k, cols), BF16)
    copy.wait()
    top = None
    for r, block in enumerate(blocks):
        lhs = jnp.concatenate([block[j] for j in range(slots)], axis=1)
        order = [j + slots * e for j in range(slots) for e in range(2)]
        rhs = jnp.concatenate([held[where_s[r, 0, o]] for o in order], axis=0)
        term = dot(lhs, rhs)
        top = term if top is None else top + term
    top = top.astype(BF16)
    for m in range(par_ref.shape[0]):
        mid[m] = dot(par_ref[m], top).astype(BF16)

    rows = send_ref.shape[1]
    for l in range(near_ref.shape[0]):
        field = leaf_ref[l] + dot(child_ref[l], mid[l // 8])
        part = (near_ref[l] + dot(basis_ref[l], field.astype(BF16))).astype(BF16)
        quarter = [part[rows * i : rows * (i + 1)] for i in range(4)]
        even = jnp.concatenate([quarter[0], quarter[2]], axis=1)
        odd = jnp.concatenate([quarter[1], quarter[3]], axis=1)
        keep_ref[l] = jnp.where(core == 0, even, odd)
        send_ref[l] = jnp.where(core == 0, odd, even)


def join(pos, upper, other, coupling, parent, leaf_part, near_part, child, basis):
    n, p, c = near_part.shape
    k = parent.shape[1]
    out = jax.ShapeDtypeStruct((n, p // 4, 2 * c), BF16)
    return pl.pallas_call(
        join_kernel,
        out_shape=(out, out),
        in_specs=[SMEM] + [VMEM] * 11,
        out_specs=(VMEM, VMEM),
        scratch_shapes=[
            pltpu.VMEM((2 * upper.shape[0] + 1, k, c), BF16),
            pltpu.VMEM((parent.shape[0], k, c), BF16),
            pltpu.VMEM((4, 8, 128), jnp.int32),
            pltpu.SMEM((4, 8, 128), jnp.int32),
            pltpu.SemaphoreType.DMA,
        ],
        compiler_params=params(8),
        cost_estimate=cost(2.0),
        name="join",
    )(pos, upper, other, *coupling, parent, leaf_part, near_part, child, basis)


def half_kernel(s_ref, keep_ref, recv_ref, send_ref, own_ref):
    c = keep_ref.shape[2] // 2
    n = keep_ref.shape[0]
    low = s_ref[0] == 0
    total = keep_ref[...].astype(F32) + recv_ref[...].astype(F32)
    first, second = total[:, :, :c], total[:, :, c:]
    own_ref[...] = jnp.where(low, first, second)
    other = jnp.where(low, second, first).astype(BF16)
    send_ref[...] = jnp.concatenate([other[: n // 2], other[n // 2 :]], axis=-1)


def half_sum(scalars, keep, recv):
    n, rows, c2 = keep.shape
    return pl.pallas_call(
        half_kernel,
        out_shape=(
            jax.ShapeDtypeStruct((n // 2, rows, c2), BF16),
            jax.ShapeDtypeStruct((n, rows, c2 // 2), F32),
        ),
        in_specs=[SMEM, VMEM, VMEM],
        out_specs=(VMEM, VMEM),
        compiler_params=params(8),
        cost_estimate=cost(0.3),
        name="half_sum",
    )(scalars, keep, recv)


def last_kernel(own_ref, recv_ref, out_ref):
    n = own_ref.shape[0]
    c = own_ref.shape[2]
    recv = recv_ref[...].astype(F32)
    out_ref[: n // 2] = (own_ref[: n // 2] + recv[:, :, :c]).astype(BF16)
    out_ref[n // 2 :] = (own_ref[n // 2 :] + recv[:, :, c:]).astype(BF16)


def last_sum(own, recv):
    return pl.pallas_call(
        last_kernel,
        out_shape=jax.ShapeDtypeStruct(own.shape, BF16),
        in_specs=[VMEM, VMEM],
        out_specs=VMEM,
        compiler_params=params(8),
        cost_estimate=cost(0.5),
        name="last_sum",
    )(own, recv)


AXES = ("leaf", "rank")


def halo_pairs(leaves):
    out = []
    for leaf in range(leaves):
        for rank in range(4):
            high = (rank & 1) != (leaf >= leaves // 2)
            to = leaf + 1 if high else leaf - 1
            if 0 <= to < leaves:
                cross = {leaf, to} == {leaves // 2 - 1, leaves // 2}
                out.append((leaf * 4 + rank, to * 4 + (rank ^ (2 if cross else 1))))
    return out


def top_pairs(step, cores):
    out = []
    for y_hi in range(2):
        for z in range(8):
            for x in range(4):
                for y_lo in range(2):
                    for core in cores:
                        s = step(y_hi, z, x, y_lo, core)
                        source = (((s[0] * 8 + s[1] % 8) * 4 + s[2]) * 2 + s[3]) * 2 + s[4]
                        out.append((source, (((y_hi * 8 + z) * 4 + x) * 2 + y_lo) * 2 + core))
    return out


def collect_upper(upper, coupling):
    def get(held, step):
        return lax.ppermute(held, AXES, top_pairs(step, (0, 1)))

    def x_step(bit):
        return lambda y_hi, z, x, y_lo, core: (y_hi, z, x ^ bit, y_lo, core)

    def z_step(bit):
        return lambda y_hi, z, x, y_lo, core: (y_hi, z ^ bit, x, y_lo, core)

    held = get(upper, lambda y_hi, z, x, y_lo, core: (y_hi ^ y_lo, z ^ (4 * core), x, y_lo, core))[None]
    held, coupling = lax.optimization_barrier((held, coupling))
    for step in (z_step(1), x_step(1), x_step(2)):
        held = jnp.concatenate([held, get(held, step)], axis=0)
    return coupling, held, get(held, z_step(2))


def shards(
    vectors,
    near_blocks,
    near_offsets,
    near_count,
    basis,
    child_transfer,
    parent_transfer,
    leaf_coupling,
    leaf_offsets,
    top_coupling,
    top_ids,
):
    leaf_dev, points, columns = vectors.shape
    leaves = lax.axis_size("leaf")
    total_leaves = leaf_dev * leaves
    leaf_pos = lax.axis_index("leaf")
    rank_pos = lax.axis_index("rank")
    core = rank_pos % 2
    y_lo = rank_pos // 2
    side = core ^ (leaf_pos >= leaves // 2)
    pos = jnp.stack([leaf_pos, rank_pos, side]).astype(jnp.int32)

    route = halo_pairs(leaves)
    swap = [(i, i ^ 1) for i in range(4)]
    own, coupling, upper, near_idx, leaf_idx = first(
        pos,
        top_ids,
        vectors,
        top_coupling[0],
        basis,
        child_transfer,
        parent_transfer,
        near_offsets.T,
        near_count[None],
        leaf_offsets.T,
        total_leaves,
    )
    halo_a = lax.ppermute(own, AXES, route)
    coupling = [coupling] + [
        lax.ppermute(coupling, "rank", [(i, i ^ bit) for i in range(4)]) for bit in (1, 2, 3)
    ]
    coupling, held, other = collect_upper(upper, coupling)
    halo_a, held = lax.optimization_barrier((halo_a, held))
    halo_b = lax.ppermute(halo_a, "rank", swap)
    near_part, leaf_part = fields(near_idx, leaf_idx, own, halo_a, halo_b, near_blocks, leaf_coupling)
    send, keep = join(
        pos, held, other, coupling, parent_transfer, leaf_part, near_part, child_transfer, basis
    )
    recv = lax.ppermute(send, "rank", swap)
    send, own = half_sum(y_lo[None].astype(jnp.int32), keep, recv)
    recv = lax.ppermute(send, "rank", [(i, i ^ 2) for i in range(4)])
    return last_sum(own, recv)


def solution(mesh):
    in_specs = (
        P("leaf", None, None),
        P("leaf", "rank", None, None),
        P("leaf", "rank"),
        P("leaf"),
        P("leaf", None, None),
        P("leaf", None, None),
        P("leaf", None, None),
        P("leaf", "rank", None, None),
        P("leaf", "rank"),
        P("leaf", "rank", None, None),
        P("leaf", "rank"),
    )
    out_specs = P("leaf", "rank", None)
    return jax.shard_map(shards, mesh=mesh, in_specs=in_specs, out_specs=out_specs, check_vma=False)
```

time: 359 us -> 61 us (0.17)
  blocking collectives: 226 us -> 0 us
  local copies, waits for them, and re-layouts: 59.2 us -> 0.04 us
  matrix products: 27.2 us -> 0 us
  starting transfers between devices: 12.8 us -> 34.1 us
  Pallas kernels: 0 us -> 15.2 us
  between operations: 13.6 us -> 0.11 us
  other arithmetic: 6.91 us -> 0.08 us
    all_gather x1 -> x0, blocking collectives: 190 us -> none  [shards(): shard_piece = lax.all_gather(upper, 'leaf', axis=0, tiled=True)]
    gather x3 -> x0, local copies, waits for them, and re-layouts: 55 us -> none  [the longest x2 33.4 us: shards(): fetched = extended[near_index]]
    psum x1 -> x0, blocking collectives: 36.2 us -> none  [shards(): lax.psum(top_part.astype(jnp.bfloat16), 'rank').astype(jnp.float32)]
    dot_general x10 -> x0, matrix products: 27.2 us -> none  [the longest x1 9.19 us: shards(): jnp.einsum('lsjk,lskr->ljr', leaf_coupling, picked, preferred_element_typ...]
    ppermute x4 -> x12, starting transfers between devices: 12.6 us -> 34.1 us  [the longest x5 21.6 us: get(): return lax.ppermute(held, AXES, top_pairs(step, (0, 1)))]
    pallas_call x0 -> x5, Pallas kernels: none -> 15.2 us  [the longest x1 7.78 us: fields(): pl.pallas_call(fields_kernel, out_shape=(out, out), in_specs=[SMEM] * 2 +...]
    reduce_scatter x1 -> x0, waiting for transfers between devices: 12.3 us -> none  [shards(): lax.psum_scatter(near_part.astype(jnp.bfloat16), 'rank', scatter_dimensio...]
    ppermute x4 -> x12, waiting for transfers between devices: 0.01 us -> 11.3 us  [the longest x5 5.31 us: get(): return lax.ppermute(held, AXES, top_pairs(step, (0, 1)))]
  transfers between devices with their start and end apart: 6 -> 12, of which waited for: 1 -> 7; matrix products, arithmetic and copies ran while one was open for 24% -> 0% of each run, Pallas kernels for 0% -> 13%
where the time goes in v2:
time: 61 us; the launch traced here: 60.8 us
  starting transfers between devices  34.1 us (56%)
  Pallas kernels  15.2 us (25%)
  waiting for transfers between devices  11.3 us (19%)
    ppermute x5, starting transfers between devices, get(): return lax.ppermute(held, AXES, top_pairs(step, (0, 1)))  21.6 us
    pallas_call x1, Pallas kernels, fields(): pl.pallas_call(fields_kernel, out_shape=(out, out), in_specs=[SMEM] * 2 +...  7.78 us
    ppermute x1, starting transfers between devices, shards(): recv = lax.ppermute(send, 'rank', [(i, i ^ 2) for i in range(4)])  5.42 us
    ppermute x5, waiting for transfers between devices, get(): return lax.ppermute(held, AXES, top_pairs(step, (0, 1)))  5.31 us
    ppermute x1, starting transfers between devices, shards(): halo_a = lax.ppermute(own, AXES, route)  4.51 us
    pallas_call x1, Pallas kernels, first(): pl.pallas_call(functools.partial(first_kernel, total=total), out_shape=(j...  3.77 us
    ppermute x1, waiting for transfers between devices, shards(): recv = lax.ppermute(send, 'rank', [(i, i ^ 2) for i in range(4)])  3.73 us
    pallas_call x1, Pallas kernels, join(): pl.pallas_call(join_kernel, out_shape=(out, out), in_specs=[SMEM] + [VMEM...  2.62 us
  transfers between devices with their start and end apart: 12, of which 7 were waited for; matrix products, arithmetic and copies ran while one was open for 0% of the time, Pallas kernels for 13%

profile of v2, /device:TPU:1, one launch (start us, length us, event | category | flops | bytes accessed | tf_op | source)
XLA Modules:
  0.0 60.8 jit_solution(378528775881647398)
XLA Ops:
  0.0 0.1 pad_add_fusion.pos_ref
  0.1 3.8 %first.1 = (bf16[64,64,128]{2,1,0:T(8,128)(2,1)S(1)}, bf16[3,64,128]{2,1,0:T(8,128)(2,1)S(1)}, bf16[32,128]{1,0:T(8,128)(2,1)S(1)}, s32[8,64]{1,0:T(8,128)S(1)}, s32[8,64]{1,0:T(8,128)S(1)}) custom-call(s32[3]{0:T(128)S(1)} %pad_add_fusion.pos_ref, bf16[64,64,64]{2,1,0:T(8,128)(2,1)} %v_any.1, bf16[64,64,64]{2,1,0:T(8,128)(2,1)} %basis_ref.1, ...), custom_call_target="tpu_custom_call" | custom-call | bytes 9000000 | tf_op jit(solution)/shard_map/first/pallas_call | solution.py:115
  3.9 4.5 %collective-permute-start = (bf16[64,64,128]{2,1,0:T(8,128)(2,1)S(1)}, bf16[64,64,128]{2,1,0:T(8,128)(2,1)S(1)}, u32[]{:S(2)}, u32[]{:S(2)}) collective-permute-start(bf16[64,64,128]{2,1,0:T(8,128)(2,1)S(1)} %get-tuple-element.23.own_ref), channel_id=1, source_target_pairs={{1,4},{3,6},{4,1},{5,8},{6,3},{7,10},{8,5},{9,12},{10,7},{11,14},{... | collective-permute-start | bytes 3145736 | tf_op jit(solution)/shard_map/ppermute | solution.py:409
  8.4 0.1 collective-permute-start.2
  8.5 1.4 %collective-permute-start.3 = (bf16[3,64,128]{2,1,0:T(8,128)(2,1)S(1)}, bf16[3,64,128]{2,1,0:T(8,128)(2,1)S(1)}, u32[]{:S(2)}, u32[]{:S(2)}) collective-permute-start(bf16[3,64,128]{2,1,0:T(8,128)(2,1)S(1)} %get-tuple-element.28.coup0_ref), channel_id=1, source_target_pairs={{0,2},{1,3},{2,0},{3,1},{4,6},{5,7},{6,4},{7,5},{8,10},{9,11},{10,... | collective-permute-start | bytes 147464 | tf_op jit(solution)/shard_map/ppermute | solution.py:411
  9.9 0.7 %collective-permute-start.4 = (bf16[3,64,128]{2,1,0:T(8,128)(2,1)S(1)}, bf16[3,64,128]{2,1,0:T(8,128)(2,1)S(1)}, u32[]{:S(2)}, u32[]{:S(2)}) collective-permute-start(bf16[3,64,128]{2,1,0:T(8,128)(2,1)S(1)} %get-tuple-element.28.coup0_ref), channel_id=1, source_target_pairs={{0,3},{1,2},{2,1},{3,0},{4,7},{5,6},{6,5},{7,4},{8,11},{9,10},{10,... | collective-permute-start | bytes 147464 | tf_op jit(solution)/shard_map/ppermute | solution.py:411
  10.6 9.0 %collective-permute-start.1 = (bf16[32,128]{1,0:T(8,128)(2,1)S(1)}, bf16[32,128]{1,0:T(8,128)(2,1)S(1)}, u32[]{:S(2)}, u32[]{:S(2)}) collective-permute-start(bf16[32,128]{1,0:T(8,128)(2,1)S(1)} %get-tuple-element.24), channel_id=1, source_target_pairs={{0,0},{65,1},{130,2},{195,3},{4,4},{69,5},{134,6},{199,7},{8,8},{7... | collective-permute-start | bytes 24584 | tf_op jit(solution)/shard_map/ppermute | solution.py:356
  19.7 1.0 %collective-permute-done.1 = bf16[32,128]{1,0:T(8,128)(2,1)S(1)} collective-permute-done((bf16[32,128]{1,0:T(8,128)(2,1)S(1)}, bf16[32,128]{1,0:T(8,128)(2,1)S(1)}, u32[]{:S(2)}, u32[]{:S(2)}) %collective-permute-start.1) | collective-permute-done | bytes 8224 | tf_op jit(solution)/shard_map/ppermute | solution.py:356
  20.7 0.0 collective-permute-done.2.coup1_ref
  20.7 0.0 collective-permute-done.3.coup2_ref
  20.7 0.0 collective-permute-done.4.coup3_ref
  20.7 1.9 %collective-permute-start.5 = (bf16[1,32,128]{2,1,0:T(8,128)(2,1)S(1)}, bf16[1,32,128]{2,1,0:T(8,128)(2,1)S(1)}, u32[]{:S(2)}, u32[]{:S(2)}) collective-permute-start(bf16[1,32,128]{2,1,0:T(8,128)(2,1)S(1)} %bitcast.9), channel_id=1, source_target_pairs={{16,0},{17,1},{18,2},{19,3},{20,4},{21,5},{22,6},{23,7},{24,8},{25... | collective-permute-start | bytes 24584 | tf_op jit(solution)/shard_map/ppermute | solution.py:356
  22.6 1.0 %collective-permute-done.5 = bf16[1,32,128]{2,1,0:T(8,128)(2,1)S(1)} collective-permute-done((bf16[1,32,128]{2,1,0:T(8,128)(2,1)S(1)}, bf16[1,32,128]{2,1,0:T(8,128)(2,1)S(1)}, u32[]{:S(2)}, u32[]{:S(2)}) %collective-permute-start.5) | collective-permute-done | bytes 8224 | tf_op jit(solution)/shard_map/ppermute | solution.py:356
  23.6 0.6 %collective-permute-start.6 = (bf16[2,32,128]{2,1,0:T(8,128)(2,1)S(1)}, bf16[2,32,128]{2,1,0:T(8,128)(2,1)S(1)}, u32[]{:S(2)}, u32[]{:S(2)}) collective-permute-start(bf16[2,32,128]{2,1,0:T(8,128)(2,1)S(1)} %pad_maximum_fusion.1), channel_id=1, source_target_pairs={{4,0},{5,1},{6,2},{7,3},{0,4},{1,5},{2,6},{3,7},{12,8},{13,9},{14,... | collective-permute-start | bytes 49160 | tf_op jit(solution)/shard_map/ppermute | solution.py:356
  24.3 1.9 %collective-permute-done.6 = bf16[2,32,128]{2,1,0:T(8,128)(2,1)S(1)} collective-permute-done((bf16[2,32,128]{2,1,0:T(8,128)(2,1)S(1)}, bf16[2,32,128]{2,1,0:T(8,128)(2,1)S(1)}, u32[]{:S(2)}, u32[]{:S(2)}) %collective-permute-start.6) | collective-permute-done | bytes 16416 | tf_op jit(solution)/shard_map/ppermute | solution.py:356
  26.2 8.3 %collective-permute-start.7 = (bf16[4,32,128]{2,1,0:T(8,128)(2,1)S(1)}, bf16[4,32,128]{2,1,0:T(8,128)(2,1)S(1)}, u32[]{:S(2)}, u32[]{:S(2)}) collective-permute-start(bf16[4,32,128]{2,1,0:T(8,128)(2,1)S(1)} %pad_maximum_fusion), channel_id=1, source_target_pairs={{8,0},{9,1},{10,2},{11,3},{12,4},{13,5},{14,6},{15,7},{0,8},{1,9},... | collective-permute-start | bytes 98312 | tf_op jit(solution)/shard_map/ppermute | solution.py:356
  34.5 1.3 %collective-permute-done.7 = bf16[4,32,128]{2,1,0:T(8,128)(2,1)S(1)} collective-permute-done((bf16[4,32,128]{2,1,0:T(8,128)(2,1)S(1)}, bf16[4,32,128]{2,1,0:T(8,128)(2,1)S(1)}, u32[]{:S(2)}, u32[]{:S(2)}) %collective-permute-start.7) | collective-permute-done | bytes 32800 | tf_op jit(solution)/shard_map/ppermute | solution.py:356
  35.8 0.0 collective-permute-done.a_ref
  35.8 0.1 collective-permute-start.9
  35.9 1.8 %collective-permute-start.8 = (bf16[8,32,128]{2,1,0:T(8,128)(2,1)S(1)}, bf16[8,32,128]{2,1,0:T(8,128)(2,1)S(1)}, u32[]{:S(2)}, u32[]{:S(2)}) collective-permute-start(bf16[8,32,128]{2,1,0:T(8,128)(2,1)S(1)} %constant_dynamic-update-slice_fusion.up_ref), channel_id=1, source_target_pairs={{32,0},{33,1},{34,2},{35,3},{36,4},{37,5},{38,6},{39,7},{40,8},{41... | collective-permute-start | bytes 196616 | tf_op jit(solution)/shard_map/ppermute | solution.py:356
  37.7 0.8 %collective-permute-done.9.b_ref = bf16[64,64,128]{2,1,0:T(8,128)(2,1)S(1)} collective-permute-done((bf16[64,64,128]{2,1,0:T(8,128)(2,1)S(1)}, bf16[64,64,128]{2,1,0:T(8,128)(2,1)S(1)}, u32[]{:S(2)}, u32[]{:S(2)}) %collective-permute-start.9) | collective-permute-done | bytes 1048608 | tf_op jit(solution)/shard_map/ppermute | solution.py:415
  38.5 7.8 %fields.1 = (f32[64,64,64]{2,1,0:T(8,128)S(1)}, f32[64,64,64]{2,1,0:T(8,128)S(1)}) custom-call(s32[8,64]{1,0:T(8,128)S(1)} %get-tuple-element.32.near_idx, s32[8,64]{1,0:T(8,128)S(1)} %get-tuple-element.33.leaf_idx, bf16[64,64,128]{2,1,0:T(8,128)(2,1)S(1)} %get-tuple-element.23.own_ref, bf16[64,64,128]{2,1,0:T(8,128)(2,1)S(1)} %collective-permute-done.a_ref, ...), custom_call_target="tpu_custom_call" | custom-call | bytes 24000000 | tf_op jit(solution)/shard_map/fields/pallas_call | solution.py:191
  46.3 0.0 collective-permute-done.8.other_ref
  46.3 0.0 copy-done
  46.3 0.0 copy-done.1
  46.4 2.6 %join.1 = (bf16[64,16,128]{2,1,0:T(8,128)(2,1)S(1)}, bf16[64,16,128]{2,1,0:T(8,128)(2,1)S(1)}) custom-call(s32[3]{0:T(128)S(1)} %pad_add_fusion.pos_ref, bf16[8,32,128]{2,1,0:T(8,128)(2,1)S(1)} %constant_dynamic-update-slice_fusion.up_ref, bf16[8,32,128]{2,1,0:T(8,128)(2,1)S(1)} %collective-permute-done.8.other_ref, ...), custom_call_target="tpu_custom_call" | custom-call | bytes 6000000 | tf_op jit(solution)/shard_map/join/pallas_call | solution.py:261
  49.0 0.2 collective-permute-start.10
  49.2 1.4 %collective-permute-done.10.recv_ref = bf16[64,16,128]{2,1,0:T(8,128)(2,1)S(1)} collective-permute-done((bf16[64,16,128]{2,1,0:T(8,128)(2,1)S(1)}, bf16[64,16,128]{2,1,0:T(8,128)(2,1)S(1)}, u32[]{:S(2)}, u32[]{:S(2)}) %collective-permute-start.10) | collective-permute-done | bytes 262176 | tf_op jit(solution)/shard_map/ppermute | solution.py:420
  50.6 0.2 half_sum.1
  50.9 5.4 %collective-permute-start.11 = (bf16[32,16,128]{2,1,0:T(8,128)(2,1)S(1)}, bf16[32,16,128]{2,1,0:T(8,128)(2,1)S(1)}, u32[]{:S(2)}, u32[]{:S(2)}) collective-permute-start(bf16[32,16,128]{2,1,0:T(8,128)(2,1)S(1)} %get-tuple-element.40), channel_id=1, source_target_pairs={{0,2},{1,3},{2,0},{3,1},{4,6},{5,7},{6,4},{7,5},{8,10},{9,11},{10,... | collective-permute-start | bytes 393224 | tf_op jit(solution)/shard_map/ppermute | solution.py:422
  56.3 3.7 %collective-permute-done.11.recv_ref = bf16[32,16,128]{2,1,0:T(8,128)(2,1)S(1)} collective-permute-done((bf16[32,16,128]{2,1,0:T(8,128)(2,1)S(1)}, bf16[32,16,128]{2,1,0:T(8,128)(2,1)S(1)}, u32[]{:S(2)}, u32[]{:S(2)}) %collective-permute-start.11) | collective-permute-done | bytes 131104 | tf_op jit(solution)/shard_map/ppermute | solution.py:422
  60.0 0.8 %last_sum.1 = bf16[64,16,64]{2,1,0:T(8,128)(2,1)} custom-call(f32[64,16,64]{2,1,0:T(8,128)S(1)} %get-tuple-element.39.own_ref, bf16[32,16,128]{2,1,0:T(8,128)(2,1)S(1)} %collective-permute-done.11.recv_ref), custom_call_target="tpu_custom_call" | custom-call | bytes 1500000 | tf_op jit(solution)/shard_map/last_sum/pallas_call | solution.py:315
  (10 shorter events, 0.0 us)
Async XLA Ops:
  3.9 31.9 %collective-permute-start = (bf16[64,64,128]{2,1,0:T(8,128)(2,1)S(1)}, bf16[64,64,128]{2,1,0:T(8,128)(2,1)S(1)}, u32[]{:S(2)}, u32[]{:S(2)}) collective-permute-start(bf16[64,64,128]{2,1,0:T(8,128)(2,1)S(1)} %get-tuple-element.23.own_ref), channel_id=1, source_target_pairs={{1,4},{3,6},{4,1},{5,8},{6,3},{7,10},{8,5},{9,12},{10,7},{11,14},{... | collective-permute-start | bytes 3145736 | tf_op jit(solution)/shard_map/ppermute | solution.py:409
  8.4 12.3 %collective-permute-start.2 = (bf16[3,64,128]{2,1,0:T(8,128)(2,1)S(1)}, bf16[3,64,128]{2,1,0:T(8,128)(2,1)S(1)}, u32[]{:S(2)}, u32[]{:S(2)}) collective-permute-start(bf16[3,64,128]{2,1,0:T(8,128)(2,1)S(1)} %get-tuple-element.28.coup0_ref), channel_id=1, source_target_pairs={{0,1},{1,0},{2,3},{3,2},{4,5},{5,4},{6,7},{7,6},{8,9},{9,8},{10,11... | collective-permute-start | bytes 147464 | tf_op jit(solution)/shard_map/ppermute | solution.py:411
  8.5 12.2 %collective-permute-start.3 = (bf16[3,64,128]{2,1,0:T(8,128)(2,1)S(1)}, bf16[3,64,128]{2,1,0:T(8,128)(2,1)S(1)}, u32[]{:S(2)}, u32[]{:S(2)}) collective-permute-start(bf16[3,64,128]{2,1,0:T(8,128)(2,1)S(1)} %get-tuple-element.28.coup0_ref), channel_id=1, source_target_pairs={{0,2},{1,3},{2,0},{3,1},{4,6},{5,7},{6,4},{7,5},{8,10},{9,11},{10,... | collective-permute-start | bytes 147464 | tf_op jit(solution)/shard_map/ppermute | solution.py:411
  9.9 10.8 %collective-permute-start.4 = (bf16[3,64,128]{2,1,0:T(8,128)(2,1)S(1)}, bf16[3,64,128]{2,1,0:T(8,128)(2,1)S(1)}, u32[]{:S(2)}, u32[]{:S(2)}) collective-permute-start(bf16[3,64,128]{2,1,0:T(8,128)(2,1)S(1)} %get-tuple-element.28.coup0_ref), channel_id=1, source_target_pairs={{0,3},{1,2},{2,1},{3,0},{4,7},{5,6},{6,5},{7,4},{8,11},{9,10},{10,... | collective-permute-start | bytes 147464 | tf_op jit(solution)/shard_map/ppermute | solution.py:411
  10.6 10.1 %collective-permute-start.1 = (bf16[32,128]{1,0:T(8,128)(2,1)S(1)}, bf16[32,128]{1,0:T(8,128)(2,1)S(1)}, u32[]{:S(2)}, u32[]{:S(2)}) collective-permute-start(bf16[32,128]{1,0:T(8,128)(2,1)S(1)} %get-tuple-element.24), channel_id=1, source_target_pairs={{0,0},{65,1},{130,2},{195,3},{4,4},{69,5},{134,6},{199,7},{8,8},{7... | collective-permute-start | bytes 24584 | tf_op jit(solution)/shard_map/ppermute | solution.py:356
  20.7 2.9 %collective-permute-start.5 = (bf16[1,32,128]{2,1,0:T(8,128)(2,1)S(1)}, bf16[1,32,128]{2,1,0:T(8,128)(2,1)S(1)}, u32[]{:S(2)}, u32[]{:S(2)}) collective-permute-start(bf16[1,32,128]{2,1,0:T(8,128)(2,1)S(1)} %bitcast.9), channel_id=1, source_target_pairs={{16,0},{17,1},{18,2},{19,3},{20,4},{21,5},{22,6},{23,7},{24,8},{25... | collective-permute-start | bytes 24584 | tf_op jit(solution)/shard_map/ppermute | solution.py:356
  23.6 2.6 %collective-permute-start.6 = (bf16[2,32,128]{2,1,0:T(8,128)(2,1)S(1)}, bf16[2,32,128]{2,1,0:T(8,128)(2,1)S(1)}, u32[]{:S(2)}, u32[]{:S(2)}) collective-permute-start(bf16[2,32,128]{2,1,0:T(8,128)(2,1)S(1)} %pad_maximum_fusion.1), channel_id=1, source_target_pairs={{4,0},{5,1},{6,2},{7,3},{0,4},{1,5},{2,6},{3,7},{12,8},{13,9},{14,... | collective-permute-start | bytes 49160 | tf_op jit(solution)/shard_map/ppermute | solution.py:356
  26.2 9.6 %collective-permute-start.7 = (bf16[4,32,128]{2,1,0:T(8,128)(2,1)S(1)}, bf16[4,32,128]{2,1,0:T(8,128)(2,1)S(1)}, u32[]{:S(2)}, u32[]{:S(2)}) collective-permute-start(bf16[4,32,128]{2,1,0:T(8,128)(2,1)S(1)} %pad_maximum_fusion), channel_id=1, source_target_pairs={{8,0},{9,1},{10,2},{11,3},{12,4},{13,5},{14,6},{15,7},{0,8},{1,9},... | collective-permute-start | bytes 98312 | tf_op jit(solution)/shard_map/ppermute | solution.py:356
  35.8 2.7 %collective-permute-start.9 = (bf16[64,64,128]{2,1,0:T(8,128)(2,1)S(1)}, bf16[64,64,128]{2,1,0:T(8,128)(2,1)S(1)}, u32[]{:S(2)}, u32[]{:S(2)}) collective-permute-start(bf16[64,64,128]{2,1,0:T(8,128)(2,1)S(1)} %collective-permute-done.a_ref), channel_id=1, source_target_pairs={{0,1},{1,0},{2,3},{3,2},{4,5},{5,4},{6,7},{7,6},{8,9},{9,8},{10,11... | collective-permute-start | bytes 3145736 | tf_op jit(solution)/shard_map/ppermute | solution.py:415
  35.9 10.4 %collective-permute-start.8 = (bf16[8,32,128]{2,1,0:T(8,128)(2,1)S(1)}, bf16[8,32,128]{2,1,0:T(8,128)(2,1)S(1)}, u32[]{:S(2)}, u32[]{:S(2)}) collective-permute-start(bf16[8,32,128]{2,1,0:T(8,128)(2,1)S(1)} %constant_dynamic-update-slice_fusion.up_ref), channel_id=1, source_target_pairs={{32,0},{33,1},{34,2},{35,3},{36,4},{37,5},{38,6},{39,7},{40,8},{41... | collective-permute-start | bytes 196616 | tf_op jit(solution)/shard_map/ppermute | solution.py:356
  38.5 7.8 %copy-start = (bf16[64,64,64]{2,1,0:T(8,128)(2,1)S(1)}, bf16[64,64,64]{2,1,0:T(8,128)(2,1)}, u32[]{:S(2)}) copy-start(bf16[64,64,64]{2,1,0:T(8,128)(2,1)} %basis_ref.1) | copy-start | bytes 1572868
  38.5 7.8 %copy-start.1 = (bf16[64,64,64]{2,1,0:T(8,128)(2,1)S(1)}, bf16[64,64,64]{2,1,0:T(8,128)(2,1)}, u32[]{:S(2)}) copy-start(bf16[64,64,64]{2,1,0:T(8,128)(2,1)} %child_ref.1) | copy-start | bytes 1572868
  38.5 7.8 %copy-start.2 = (bf16[8,64,64]{2,1,0:T(8,128)(2,1)S(1)}, bf16[8,64,64]{2,1,0:T(8,128)(2,1)}, u32[]{:S(2)}) copy-start(bf16[8,64,64]{2,1,0:T(8,128)(2,1)} %par_ref.1) | copy-start | bytes 196612
  49.0 1.6 %collective-permute-start.10 = (bf16[64,16,128]{2,1,0:T(8,128)(2,1)S(1)}, bf16[64,16,128]{2,1,0:T(8,128)(2,1)S(1)}, u32[]{:S(2)}, u32[]{:S(2)}) collective-permute-start(bf16[64,16,128]{2,1,0:T(8,128)(2,1)S(1)} %get-tuple-element.38), channel_id=1, source_target_pairs={{0,1},{1,0},{2,3},{3,2},{4,5},{5,4},{6,7},{7,6},{8,9},{9,8},{10,11... | collective-permute-start | bytes 786440 | tf_op jit(solution)/shard_map/ppermute | solution.py:420
  50.9 9.2 %collective-permute-start.11 = (bf16[32,16,128]{2,1,0:T(8,128)(2,1)S(1)}, bf16[32,16,128]{2,1,0:T(8,128)(2,1)S(1)}, u32[]{:S(2)}, u32[]{:S(2)}) collective-permute-start(bf16[32,16,128]{2,1,0:T(8,128)(2,1)S(1)} %get-tuple-element.40), channel_id=1, source_target_pairs={{0,2},{1,3},{2,0},{3,1},{4,6},{5,7},{6,4},{7,5},{8,10},{9,11},{10,... | collective-permute-start | bytes 393224 | tf_op jit(solution)/shard_map/ppermute | solution.py:422

commit v3 on v2

--- a/solution.py
+++ b/solution.py
@@ -47,9 +47,9 @@
 
 
 def first_kernel(
-    pos_ref, v_any, b_any, c_any, p_any, t_any, ids_any, near_any, count_any, leaf_any,
-    out_ref, coup_ref, up_ref, near_idx, leaf_idx,
-    v, b, c, p, t, ids, near, count, leaf, mid, sems, *, total,
+    pos_ref, v_any, b_any, c_any, p_any, near_any, count_any, leaf_any, t_any, ids_any,
+    out_ref, up_ref, near_idx, leaf_idx, c0_ref, c1_ref, c2_ref, c3_ref,
+    v, b, c, p, near, count, leaf, t, ids, mid, sems, *, total,
 ):
     copies = load(
         (v_any, b_any, c_any, p_any, near_any, count_any, leaf_any, t_any, ids_any),
@@ -76,12 +76,18 @@
     here = mid[...].reshape(mids * k, 2 * cols)
     low = dot_t(p[:mids].reshape(mids * k, k), here)
     high = dot_t(p[mids:].reshape(mids * k, k), here)
-    up = (low[:, :cols] + high[:, cols:]).astype(BF16)
-    up_ref[...] = jnp.concatenate([up[: k // 2], up[k // 2 :]], axis=-1)
+    up = low[:, :cols] + high[:, cols:]
+    rank = pos_ref[1]
+    piece = k // 4
+    quarter = up[:piece]
+    for r in range(1, 4):
+        quarter = jnp.where(rank == r, up[piece * r : piece * (r + 1)], quarter)
+    quarter = jnp.concatenate([quarter[: piece // 2], quarter[piece // 2 :]], axis=-1).astype(BF16)
+    for i in range(up_ref.shape[0]):
+        up_ref[i] = quarter
 
     slots = near.shape[0]
     own_first = pos_ref[0] * n
-    rank = pos_ref[1]
     side = pos_ref[2]
     leaf_ids = own_first + lax.broadcasted_iota(jnp.int32, near.shape, 1)
 
@@ -97,45 +103,55 @@
     near_idx[...] = jnp.where(slot < count[...], place(near[...]), 3 * n)
     leaf_idx[...] = place(leaf[...])
 
-    top_slots = t.shape[0] // 2
-    coup_ref[:top_slots] = jnp.concatenate([t[:top_slots], t[top_slots:]], axis=-1)
-    lane = lax.broadcasted_iota(jnp.int32, coup_ref.shape[1:], 1)
-    row = jnp.zeros(coup_ref.shape[1:], F32)
-    for s in range(2 * top_slots):
+    top_slots = t.shape[0]
+    columns = []
+    for r in range(4):
+        part = jnp.concatenate([t[s, :, piece * r : piece * (r + 1)] for s in range(top_slots)], axis=1)
+        columns.append(jnp.concatenate([part[: k // 2], part[k // 2 :]], axis=1))
+    lane = lax.broadcasted_iota(jnp.int32, (16, 2 * k), 1)
+    row = jnp.zeros((16, 2 * k), F32)
+    for s in range(top_slots):
         row = jnp.where(lane == s, ids[0, s].astype(F32), row)
-    coup_ref[top_slots] = row.astype(BF16)
-
-
-def first(pos, ids, vectors, coupling, basis, child, parent, near_offsets, near_count, leaf_offsets, total):
+    for bit, ref in enumerate((c0_ref, c1_ref, c2_ref, c3_ref)):
+        to = rank ^ bit
+        part = columns[0]
+        for r in range(1, 4):
+            part = jnp.where(to == r, columns[r], part)
+        ref[: k // 2] = part
+        ref[k // 2 :] = row.astype(BF16)
+
+
+def first(pos, vectors, basis, child, parent, near_offsets, near_count, leaf_offsets, coupling, ids, total):
     n, p, c = vectors.shape
     k = basis.shape[2]
-    sources = (vectors, basis, child, parent, coupling)
-    small = (ids, near_offsets, near_count, leaf_offsets)
+    sources = (vectors, basis, child, parent)
+    small = (near_offsets, near_count, leaf_offsets)
     shape = near_offsets.shape
     return pl.pallas_call(
         functools.partial(first_kernel, total=total),
         out_shape=(
             jax.ShapeDtypeStruct((n, p, 2 * c), BF16),
-            jax.ShapeDtypeStruct((coupling.shape[0] // 2 + 1, k, 2 * k), BF16),
-            jax.ShapeDtypeStruct((k // 2, 2 * c), BF16),
+            jax.ShapeDtypeStruct((total // n, k // 8, 2 * c), BF16),
             jax.ShapeDtypeStruct(shape, jnp.int32),
             jax.ShapeDtypeStruct(shape, jnp.int32),
-        ),
+        )
+        + (jax.ShapeDtypeStruct((k // 2 + 16, 2 * k), BF16),) * 4,
         in_specs=[SMEM] + [pl.BlockSpec(memory_space=pltpu.HBM)] * 9,
-        out_specs=(VMEM,) * 5,
+        out_specs=(VMEM,) * 8,
         scratch_shapes=[pltpu.VMEM(a.shape, BF16) for a in sources]
         + [
-            pltpu.SMEM(ids.shape, jnp.int32),
             pltpu.VMEM(shape, jnp.int32),
             pltpu.VMEM(near_count.shape, jnp.int32),
             pltpu.VMEM(shape, jnp.int32),
+            pltpu.VMEM(coupling.shape, BF16),
+            pltpu.SMEM(ids.shape, jnp.int32),
             pltpu.VMEM((n // 16, k, 2 * c), BF16),
             pltpu.SemaphoreType.DMA((9,)),
         ],
         compiler_params=params(16),
         cost_estimate=cost(3.0),
         name="first",
-    )(pos, *pinned(*sources, *small))
+    )(pos, *pinned(*sources, *small, coupling, ids))
 
 
 CHUNK = 8
@@ -207,38 +223,26 @@
 
 
 def join_kernel(
-    pos_ref, up_ref, other_ref, coup0_ref, coup1_ref, coup2_ref, coup3_ref, par_ref, leaf_ref, near_ref, child_ref, basis_ref,
-    send_ref, keep_ref, held, mid, where_v, where_s, sem,
+    pos_ref, up_ref, c0_ref, c1_ref, c2_ref, c3_ref, par_ref, leaf_ref, near_ref, child_ref, basis_ref,
+    send_ref, keep_ref, mid, ids_v, ids_s, sem,
 ):
+    cols = near_ref.shape[2]
     k = par_ref.shape[1]
-    cols = near_ref.shape[2]
-    half = up_ref.shape[0]
-    count = 2 * half
-    leaf_pos, rank = pos_ref[0], pos_ref[1]
-    core = rank & 1
-    blocks = (coup0_ref, coup1_ref, coup2_ref, coup3_ref)
-    slots = coup0_ref.shape[0] - 1
-    for r, block in enumerate(blocks):
-        ids = block[slots, :16].astype(F32).astype(jnp.int32)[:8]
-        dz = ((ids >> 2) & 7) ^ ((leaf_pos >> 2) & 7) ^ (4 * core)
-        dx = (ids & 3) ^ (leaf_pos & 3)
-        here = ((ids >> 5) == ((leaf_pos >> 5) ^ (rank >> 1))) & (dz < 4)
-        where_v[r] = jnp.where(here, (dz & 1) + 2 * dx + 8 * (dz >> 1), count)
-    copy = pltpu.make_async_copy(where_v, where_s, sem)
+    core = pos_ref[1] & 1
+    parts = (c0_ref, c1_ref, c2_ref, c3_ref)
+    for b, ref in enumerate(parts):
+        ids_v[b] = ref[k // 2 :].astype(F32).astype(jnp.int32)[:8]
+    copy = pltpu.make_async_copy(ids_v, ids_s, sem)
     copy.start()
-    for start, ref in ((0, up_ref), (half, other_ref)):
-        for i in range(half):
-            held[start + i, : k // 2] = ref[i, :, :cols]
-            held[start + i, k // 2 :] = ref[i, :, cols:]
-    held[count] = jnp.zeros((k, cols), BF16)
+    lhs = [ref[: k // 2] for ref in parts]
+    lhs = jnp.concatenate([jnp.concatenate([c[:, :k], c[:, k:]], axis=0) for c in lhs], axis=1)
     copy.wait()
-    top = None
-    for r, block in enumerate(blocks):
-        lhs = jnp.concatenate([block[j] for j in range(slots)], axis=1)
-        order = [j + slots * e for j in range(slots) for e in range(2)]
-        rhs = jnp.concatenate([held[where_s[r, 0, o]] for o in order], axis=0)
-        term = dot(lhs, rhs)
-        top = term if top is None else top + term
+    rhs = []
+    for b in range(4):
+        for s in range(4):
+            u = up_ref[ids_s[b, 0, s]].astype(F32)
+            rhs += [u[:, :cols], u[:, cols:]]
+    top = dot(lhs, jnp.concatenate(rhs, axis=0).astype(BF16))
     top = top.astype(BF16)
     for m in range(par_ref.shape[0]):
         mid[m] = dot(par_ref[m], top).astype(BF16)
@@ -254,26 +258,25 @@
         send_ref[l] = jnp.where(core == 0, odd, even)
 
 
-def join(pos, upper, other, coupling, parent, leaf_part, near_part, child, basis):
+def join(pos, upper, coupling, parent, leaf_part, near_part, child, basis):
     n, p, c = near_part.shape
     k = parent.shape[1]
     out = jax.ShapeDtypeStruct((n, p // 4, 2 * c), BF16)
     return pl.pallas_call(
         join_kernel,
         out_shape=(out, out),
-        in_specs=[SMEM] + [VMEM] * 11,
+        in_specs=[SMEM] + [VMEM] * 10,
         out_specs=(VMEM, VMEM),
         scratch_shapes=[
-            pltpu.VMEM((2 * upper.shape[0] + 1, k, c), BF16),
             pltpu.VMEM((parent.shape[0], k, c), BF16),
-            pltpu.VMEM((4, 8, 128), jnp.int32),
-            pltpu.SMEM((4, 8, 128), jnp.int32),
+            pltpu.VMEM((4, 8, 2 * k), jnp.int32),
+            pltpu.SMEM((4, 8, 2 * k), jnp.int32),
             pltpu.SemaphoreType.DMA,
         ],
         compiler_params=params(8),
         cost_estimate=cost(2.0),
         name="join",
-    )(pos, upper, other, *coupling, parent, leaf_part, near_part, child, basis)
+    )(pos, upper, *coupling, parent, leaf_part, near_part, child, basis)
 
 
 def half_kernel(s_ref, keep_ref, recv_ref, send_ref, own_ref):
@@ -336,36 +339,6 @@
                 cross = {leaf, to} == {leaves // 2 - 1, leaves // 2}
                 out.append((leaf * 4 + rank, to * 4 + (rank ^ (2 if cross else 1))))
     return out
-
-
-def top_pairs(step, cores):
-    out = []
-    for y_hi in range(2):
-        for z in range(8):
-            for x in range(4):
-                for y_lo in range(2):
-                    for core in cores:
-                        s = step(y_hi, z, x, y_lo, core)
-                        source = (((s[0] * 8 + s[1] % 8) * 4 + s[2]) * 2 + s[3]) * 2 + s[4]
-                        out.append((source, (((y_hi * 8 + z) * 4 + x) * 2 + y_lo) * 2 + core))
-    return out
-
-
-def collect_upper(upper, coupling):
-    def get(held, step):
-        return lax.ppermute(held, AXES, top_pairs(step, (0, 1)))
-
-    def x_step(bit):
-        return lambda y_hi, z, x, y_lo, core: (y_hi, z, x ^ bit, y_lo, core)
-
-    def z_step(bit):
-        return lambda y_hi, z, x, y_lo, core: (y_hi, z ^ bit, x, y_lo, core)
-
-    held = get(upper, lambda y_hi, z, x, y_lo, core: (y_hi ^ y_lo, z ^ (4 * core), x, y_lo, core))[None]
-    held, coupling = lax.optimization_barrier((held, coupling))
-    for step in (z_step(1), x_step(1), x_step(2)):
-        held = jnp.concatenate([held, get(held, step)], axis=0)
-    return coupling, held, get(held, z_step(2))
 
 
 def shards(
@@ -393,29 +366,29 @@
 
     route = halo_pairs(leaves)
     swap = [(i, i ^ 1) for i in range(4)]
-    own, coupling, upper, near_idx, leaf_idx = first(
+    own, upper, near_idx, leaf_idx, *coupling = first(
         pos,
-        top_ids,
         vectors,
-        top_coupling[0],
         basis,
         child_transfer,
         parent_transfer,
         near_offsets.T,
         near_count[None],
         leaf_offsets.T,
+        top_coupling[0],
+        top_ids,
         total_leaves,
     )
     halo_a = lax.ppermute(own, AXES, route)
-    coupling = [coupling] + [
-        lax.ppermute(coupling, "rank", [(i, i ^ bit) for i in range(4)]) for bit in (1, 2, 3)
+    upper = lax.all_to_all(upper, "leaf", 0, 0)
+    halo_a, upper, coupling = lax.optimization_barrier((halo_a, upper, coupling))
+    halo_b = lax.ppermute(halo_a, "rank", swap)
+    coupling = coupling[:1] + [
+        lax.ppermute(coupling[bit], "rank", [(i, i ^ bit) for i in range(4)]) for bit in (1, 2, 3)
     ]
-    coupling, held, other = collect_upper(upper, coupling)
-    halo_a, held = lax.optimization_barrier((halo_a, held))
-    halo_b = lax.ppermute(halo_a, "rank", swap)
     near_part, leaf_part = fields(near_idx, leaf_idx, own, halo_a, halo_b, near_blocks, leaf_coupling)
     send, keep = join(
-        pos, held, other, coupling, parent_transfer, leaf_part, near_part, child_transfer, basis
+        pos, upper, coupling, parent_transfer, leaf_part, near_part, child_transfer, basis
     )
     recv = lax.ppermute(send, "rank", swap)
     send, own = half_sum(y_lo[None].astype(jnp.int32), keep, recv)

time: 61 us -> 55.5 us (0.910)
  blocking collectives: 0 us -> 24.6 us
  starting transfers between devices: 34.1 us -> 9.6 us
  waiting for transfers between devices: 11.3 us -> 5.63 us
    all_to_all x0 -> x1, blocking collectives: none -> 24.6 us  [shards(): upper = lax.all_to_all(upper, 'leaf', 0, 0)]
    ppermute x8 -> x3, starting transfers between devices: 23.8 us -> 2.14 us  [shards(): lax.ppermute(coupling[bit], 'rank', [(i, i ^ bit) for i in range(4)])]
    ppermute x8 -> x3, waiting for transfers between devices: 5.32 us -> 0.01 us  [shards(): lax.ppermute(coupling[bit], 'rank', [(i, i ^ bit) for i in range(4)])]
    ppermute x1, starting transfers between devices: 5.42 us -> 0.49 us  [shards(): recv = lax.ppermute(send, 'rank', [(i, i ^ 2) for i in range(4)])]
    ppermute x1, starting transfers between devices: 0.09 us -> 2.01 us  [shards(): halo_b = lax.ppermute(halo_a, 'rank', swap)]
    ppermute x1, waiting for transfers between devices: 0.83 us -> 0.14 us  [shards(): halo_b = lax.ppermute(halo_a, 'rank', swap)]
  transfers between devices with their start and end apart: 12 -> 7, of which waited for: 7 -> 3; matrix products, arithmetic and copies ran while one was open for 0% -> 0% of each run, Pallas kernels for 13% -> 14%
where the time goes in v3:
time: 55.5 us; the launch traced here: 55.3 us
  blocking collectives  24.6 us (44%)
  Pallas kernels  15.3 us (28%)
  starting transfers between devices  9.6 us (17%)
  waiting for transfers between devices  5.63 us (10%)
    all_to_all x1, blocking collectives, shards(): upper = lax.all_to_all(upper, 'leaf', 0, 0)  24.6 us
    pallas_call x1, Pallas kernels, fields(): pl.pallas_call(fields_kernel, out_shape=(out, out), in_specs=[SMEM] * 2 +...  7.78 us
    ppermute x1, starting transfers between devices, shards(): halo_a = lax.ppermute(own, AXES, route)  4.51 us
    ppermute x1, waiting for transfers between devices, shards(): recv = lax.ppermute(send, 'rank', [(i, i ^ 2) for i in range(4)])  4.31 us
    pallas_call x1, Pallas kernels, first(): pl.pallas_call(functools.partial(first_kernel, total=total), out_shape=(j...  3.87 us
    pallas_call x1, Pallas kernels, join(): pl.pallas_call(join_kernel, out_shape=(out, out), in_specs=[SMEM] + [VMEM...  2.6 us
    ppermute x3, starting transfers between devices, shards(): lax.ppermute(coupling[bit], 'rank', [(i, i ^ bit) for i in range(4)])  2.14 us
    ppermute x1, starting transfers between devices, shards(): halo_b = lax.ppermute(halo_a, 'rank', swap)  2.01 us
  transfers between devices with their start and end apart: 7, of which 3 were waited for; matrix products, arithmetic and copies ran while one was open for 0% of the time, Pallas kernels for 14%

profile of v3, /device:TPU:1, one launch (start us, length us, event | category | flops | bytes accessed | tf_op | source)
XLA Modules:
  0.0 55.3 jit_solution(290875262913644833)
XLA Ops:
  0.0 0.1 pad_add_fusion.pos_ref
  0.1 3.9 %first.1 = (bf16[64,64,128]{2,1,0:T(8,128)(2,1)S(1)}, bf16[64,8,128]{2,1,0:T(8,128)(2,1)S(1)}, s32[8,64]{1,0:T(8,128)S(1)}, s32[8,64]{1,0:T(8,128)S(1)}, bf16[48...) custom-call(s32[3]{0:T(128)S(1)} %pad_add_fusion.pos_ref, ...), custom_call_target="tpu_custom_call" | custom-call | bytes 9000000 | tf_op jit(solution)/shard_map/first/pallas_call | solution.py:130
  4.0 4.5 %collective-permute-start = (bf16[64,64,128]{2,1,0:T(8,128)(2,1)S(1)}, bf16[64,64,128]{2,1,0:T(8,128)(2,1)S(1)}, u32[]{:S(2)}, u32[]{:S(2)}) collective-permute-start(bf16[64,64,128]{2,1,0:T(8,128)(2,1)S(1)} %get-tuple-element.25.own_ref), channel_id=1, source_target_pairs={{1,4},{3,6},{4,1},{5,8},{6,3},{7,10},{8,5},{9,12},{10,7},{11,14},{... | collective-permute-start | bytes 3145736 | tf_op jit(solution)/shard_map/ppermute | solution.py:382
  8.5 24.6 %all_to_all.5.up_ref = bf16[64,8,128]{2,1,0:T(8,128)(2,1)S(1)} all-to-all(bf16[64,8,128]{2,1,0:T(8,128)(2,1)S(1)} %get-tuple-element.26), channel_id=1, replica_groups=mesh['leaf'=64,'rank'=4] {'leaf'}, dimensions={0} | all-to-all | bytes 262144 | tf_op jit(solution)/shard_map/all_to_all | solution.py:383
  33.1 0.0 collective-permute-done.a_ref
  33.1 2.0 %collective-permute-start.4 = (bf16[64,64,128]{2,1,0:T(8,128)(2,1)S(1)}, bf16[64,64,128]{2,1,0:T(8,128)(2,1)S(1)}, u32[]{:S(2)}, u32[]{:S(2)}) collective-permute-start(bf16[64,64,128]{2,1,0:T(8,128)(2,1)S(1)} %collective-permute-done.a_ref), channel_id=1, source_target_pairs={{0,1},{1,0},{2,3},{3,2},{4,5},{5,4},{6,7},{7,6},{8,9},{9,8},{10,11... | collective-permute-start | bytes 3145736 | tf_op jit(solution)/shard_map/ppermute | solution.py:385
  35.1 0.0 collective-permute-start.1
  35.1 0.4 collective-permute-start.2
  35.5 1.7 %collective-permute-start.3 = (bf16[48,128]{1,0:T(8,128)(2,1)S(1)}, bf16[48,128]{1,0:T(8,128)(2,1)S(1)}, u32[]{:S(2)}, u32[]{:S(2)}) collective-permute-start(bf16[48,128]{1,0:T(8,128)(2,1)S(1)} %get-tuple-element.35), channel_id=1, source_target_pairs={{0,3},{1,2},{2,1},{3,0},{4,7},{5,6},{6,5},{7,4},{8,11},{9,10},{10,... | collective-permute-start | bytes 36872 | tf_op jit(solution)/shard_map/ppermute | solution.py:387
  37.3 0.1 collective-permute-done.4.b_ref
  37.4 0.0 copy-start
  37.4 0.0 copy-start.1
  37.4 0.0 copy-start.2
  37.4 7.8 %fields.1 = (f32[64,64,64]{2,1,0:T(8,128)S(1)}, f32[64,64,64]{2,1,0:T(8,128)S(1)}) custom-call(s32[8,64]{1,0:T(8,128)S(1)} %get-tuple-element.36.near_idx, s32[8,64]{1,0:T(8,128)S(1)} %get-tuple-element.37.leaf_idx, bf16[64,64,128]{2,1,0:T(8,128)(2,1)S(1)} %get-tuple-element.25.own_ref, bf16[64,64,128]{2,1,0:T(8,128)(2,1)S(1)} %collective-permute-done.a_ref, ...), custom_call_target="tpu_custom_call" | custom-call | bytes 24000000 | tf_op jit(solution)/shard_map/fields/pallas_call | solution.py:207
  45.2 0.0 collective-permute-done.1.c1_ref
  45.2 0.0 collective-permute-done.2.c2_ref
  45.2 0.0 collective-permute-done.3.c3_ref
  45.2 0.0 copy-done
  45.2 0.0 copy-done.1
  45.2 0.0 copy-done.2
  45.3 2.6 %join.1 = (bf16[64,16,128]{2,1,0:T(8,128)(2,1)S(1)}, bf16[64,16,128]{2,1,0:T(8,128)(2,1)S(1)}) custom-call(s32[3]{0:T(128)S(1)} %pad_add_fusion.pos_ref, bf16[64,8,128]{2,1,0:T(8,128)(2,1)S(1)} %all_to_all.5.up_ref, bf16[48,128]{1,0:T(8,128)(2,1)S(1)} %get-tuple-element.32.c0_ref, bf16[48,128]{1,0:T(8,128)(2,1)S(1)} %collective-permute-done.1.c1_ref, ...), custom_call_target="tpu_custom_call" | custom-call | bytes 6000000 | tf_op jit(solution)/shard_map/join/pallas_call | solution.py:265
  47.9 0.5 collective-permute-start.5
  48.3 1.2 %collective-permute-done.5.recv_ref = bf16[64,16,128]{2,1,0:T(8,128)(2,1)S(1)} collective-permute-done((bf16[64,16,128]{2,1,0:T(8,128)(2,1)S(1)}, bf16[64,16,128]{2,1,0:T(8,128)(2,1)S(1)}, u32[]{:S(2)}, u32[]{:S(2)}) %collective-permute-start.5) | collective-permute-done | bytes 262176 | tf_op jit(solution)/shard_map/ppermute | solution.py:393
  49.5 0.2 half_sum.1
  49.7 0.5 collective-permute-start.6
  50.2 4.3 %collective-permute-done.6.recv_ref = bf16[32,16,128]{2,1,0:T(8,128)(2,1)S(1)} collective-permute-done((bf16[32,16,128]{2,1,0:T(8,128)(2,1)S(1)}, bf16[32,16,128]{2,1,0:T(8,128)(2,1)S(1)}, u32[]{:S(2)}, u32[]{:S(2)}) %collective-permute-start.6) | collective-permute-done | bytes 131104 | tf_op jit(solution)/shard_map/ppermute | solution.py:395
  54.5 0.8 %last_sum.1 = bf16[64,16,64]{2,1,0:T(8,128)(2,1)} custom-call(f32[64,16,64]{2,1,0:T(8,128)S(1)} %get-tuple-element.43.own_ref, bf16[32,16,128]{2,1,0:T(8,128)(2,1)S(1)} %collective-permute-done.6.recv_ref), custom_call_target="tpu_custom_call" | custom-call | bytes 1500000 | tf_op jit(solution)/shard_map/last_sum/pallas_call | solution.py:318
Async XLA Ops:
  4.0 29.1 %collective-permute-start = (bf16[64,64,128]{2,1,0:T(8,128)(2,1)S(1)}, bf16[64,64,128]{2,1,0:T(8,128)(2,1)S(1)}, u32[]{:S(2)}, u32[]{:S(2)}) collective-permute-start(bf16[64,64,128]{2,1,0:T(8,128)(2,1)S(1)} %get-tuple-element.25.own_ref), channel_id=1, source_target_pairs={{1,4},{3,6},{4,1},{5,8},{6,3},{7,10},{8,5},{9,12},{10,7},{11,14},{... | collective-permute-start | bytes 3145736 | tf_op jit(solution)/shard_map/ppermute | solution.py:382
  33.1 4.3 %collective-permute-start.4 = (bf16[64,64,128]{2,1,0:T(8,128)(2,1)S(1)}, bf16[64,64,128]{2,1,0:T(8,128)(2,1)S(1)}, u32[]{:S(2)}, u32[]{:S(2)}) collective-permute-start(bf16[64,64,128]{2,1,0:T(8,128)(2,1)S(1)} %collective-permute-done.a_ref), channel_id=1, source_target_pairs={{0,1},{1,0},{2,3},{3,2},{4,5},{5,4},{6,7},{7,6},{8,9},{9,8},{10,11... | collective-permute-start | bytes 3145736 | tf_op jit(solution)/shard_map/ppermute | solution.py:385
  35.1 10.1 %collective-permute-start.1 = (bf16[48,128]{1,0:T(8,128)(2,1)S(1)}, bf16[48,128]{1,0:T(8,128)(2,1)S(1)}, u32[]{:S(2)}, u32[]{:S(2)}) collective-permute-start(bf16[48,128]{1,0:T(8,128)(2,1)S(1)} %get-tuple-element.33), channel_id=1, source_target_pairs={{0,1},{1,0},{2,3},{3,2},{4,5},{5,4},{6,7},{7,6},{8,9},{9,8},{10,11... | collective-permute-start | bytes 36872 | tf_op jit(solution)/shard_map/ppermute | solution.py:387
  35.1 10.1 %collective-permute-start.2 = (bf16[48,128]{1,0:T(8,128)(2,1)S(1)}, bf16[48,128]{1,0:T(8,128)(2,1)S(1)}, u32[]{:S(2)}, u32[]{:S(2)}) collective-permute-start(bf16[48,128]{1,0:T(8,128)(2,1)S(1)} %get-tuple-element.34), channel_id=1, source_target_pairs={{0,2},{1,3},{2,0},{3,1},{4,6},{5,7},{6,4},{7,5},{8,10},{9,11},{10,... | collective-permute-start | bytes 36872 | tf_op jit(solution)/shard_map/ppermute | solution.py:387
  35.5 9.7 %collective-permute-start.3 = (bf16[48,128]{1,0:T(8,128)(2,1)S(1)}, bf16[48,128]{1,0:T(8,128)(2,1)S(1)}, u32[]{:S(2)}, u32[]{:S(2)}) collective-permute-start(bf16[48,128]{1,0:T(8,128)(2,1)S(1)} %get-tuple-element.35), channel_id=1, source_target_pairs={{0,3},{1,2},{2,1},{3,0},{4,7},{5,6},{6,5},{7,4},{8,11},{9,10},{10,... | collective-permute-start | bytes 36872 | tf_op jit(solution)/shard_map/ppermute | solution.py:387
  37.4 7.8 %copy-start = (bf16[64,64,64]{2,1,0:T(8,128)(2,1)S(1)}, bf16[64,64,64]{2,1,0:T(8,128)(2,1)}, u32[]{:S(2)}) copy-start(bf16[64,64,64]{2,1,0:T(8,128)(2,1)} %basis_ref.1) | copy-start | bytes 1572868
  37.4 7.8 %copy-start.1 = (bf16[64,64,64]{2,1,0:T(8,128)(2,1)S(1)}, bf16[64,64,64]{2,1,0:T(8,128)(2,1)}, u32[]{:S(2)}) copy-start(bf16[64,64,64]{2,1,0:T(8,128)(2,1)} %child_ref.1) | copy-start | bytes 1572868
  37.4 7.8 %copy-start.2 = (bf16[8,64,64]{2,1,0:T(8,128)(2,1)S(1)}, bf16[8,64,64]{2,1,0:T(8,128)(2,1)}, u32[]{:S(2)}) copy-start(bf16[8,64,64]{2,1,0:T(8,128)(2,1)} %par_ref.1) | copy-start | bytes 196612
  47.9 1.6 %collective-permute-start.5 = (bf16[64,16,128]{2,1,0:T(8,128)(2,1)S(1)}, bf16[64,16,128]{2,1,0:T(8,128)(2,1)S(1)}, u32[]{:S(2)}, u32[]{:S(2)}) collective-permute-start(bf16[64,16,128]{2,1,0:T(8,128)(2,1)S(1)} %get-tuple-element.42), channel_id=1, source_target_pairs={{0,1},{1,0},{2,3},{3,2},{4,5},{5,4},{6,7},{7,6},{8,9},{9,8},{10,11... | collective-permute-start | bytes 786440 | tf_op jit(solution)/shard_map/ppermute | solution.py:393
  49.7 4.8 %collective-permute-start.6 = (bf16[32,16,128]{2,1,0:T(8,128)(2,1)S(1)}, bf16[32,16,128]{2,1,0:T(8,128)(2,1)S(1)}, u32[]{:S(2)}, u32[]{:S(2)}) collective-permute-start(bf16[32,16,128]{2,1,0:T(8,128)(2,1)S(1)} %get-tuple-element.44), channel_id=1, source_target_pairs={{0,2},{1,3},{2,0},{3,1},{4,6},{5,7},{6,4},{7,5},{8,10},{9,11},{10,... | collective-permute-start | bytes 393224 | tf_op jit(solution)/shard_map/ppermute | solution.py:395

commit v4 on v3

--- a/solution.py
+++ b/solution.py
@@ -52,39 +52,15 @@
     v, b, c, p, near, count, leaf, t, ids, mid, sems, *, total,
 ):
     copies = load(
-        (v_any, b_any, c_any, p_any, near_any, count_any, leaf_any, t_any, ids_any),
-        (v, b, c, p, near, count, leaf, t, ids),
+        (near_any, count_any, leaf_any, t_any, ids_any, v_any, b_any, c_any, p_any),
+        (near, count, leaf, t, ids, v, b, c, p),
         sems,
     )
     n, _, k = b.shape
     cols = v.shape[2]
     half = n // 2
-    copies[0].wait()
-    out_ref[:half] = jnp.concatenate([v[:half], v[half:]], axis=-1)
-    copies[1].wait()
-    for i in range(half):
-        both = dot_t(jnp.concatenate([b[i], b[half + i]], axis=1), out_ref[i])
-        out_ref[half + i] = left_right(both[:k], both[k:]).astype(BF16)
-    copies[2].wait()
-    for m in range(n // 16):
-        here = out_ref[half + 8 * m : half + 8 * m + 8].reshape(8 * k, 2 * cols)
-        low = dot_t(c[8 * m : 8 * m + 8].reshape(8 * k, k), here)
-        high = dot_t(c[half + 8 * m : half + 8 * m + 8].reshape(8 * k, k), here)
-        mid[m] = left_right(low, high).astype(BF16)
-    copies[3].wait()
-    mids = n // 16
-    here = mid[...].reshape(mids * k, 2 * cols)
-    low = dot_t(p[:mids].reshape(mids * k, k), here)
-    high = dot_t(p[mids:].reshape(mids * k, k), here)
-    up = low[:, :cols] + high[:, cols:]
     rank = pos_ref[1]
     piece = k // 4
-    quarter = up[:piece]
-    for r in range(1, 4):
-        quarter = jnp.where(rank == r, up[piece * r : piece * (r + 1)], quarter)
-    quarter = jnp.concatenate([quarter[: piece // 2], quarter[piece // 2 :]], axis=-1).astype(BF16)
-    for i in range(up_ref.shape[0]):
-        up_ref[i] = quarter
 
     slots = near.shape[0]
     own_first = pos_ref[0] * n
@@ -98,7 +74,7 @@
         return jnp.where(rel < 0, under, jnp.where(rel >= n, over, rel))
 
     slot = rank * slots + lax.broadcasted_iota(jnp.int32, near.shape, 0)
-    for copy in copies[4:]:
+    for copy in copies[:5]:
         copy.wait()
     near_idx[...] = jnp.where(slot < count[...], place(near[...]), 3 * n)
     leaf_idx[...] = place(leaf[...])
@@ -119,6 +95,31 @@
             part = jnp.where(to == r, columns[r], part)
         ref[: k // 2] = part
         ref[k // 2 :] = row.astype(BF16)
+
+    copies[5].wait()
+    out_ref[:half] = jnp.concatenate([v[:half], v[half:]], axis=-1)
+    copies[6].wait()
+    for i in range(half):
+        both = dot_t(jnp.concatenate([b[i], b[half + i]], axis=1), out_ref[i])
+        out_ref[half + i] = left_right(both[:k], both[k:]).astype(BF16)
+    copies[7].wait()
+    for m in range(n // 16):
+        here = out_ref[half + 8 * m : half + 8 * m + 8].reshape(8 * k, 2 * cols)
+        low = dot_t(c[8 * m : 8 * m + 8].reshape(8 * k, k), here)
+        high = dot_t(c[half + 8 * m : half + 8 * m + 8].reshape(8 * k, k), here)
+        mid[m] = left_right(low, high).astype(BF16)
+    copies[8].wait()
+    mids = n // 16
+    here = mid[...].reshape(mids * k, 2 * cols)
+    low = dot_t(p[:mids].reshape(mids * k, k), here)
+    high = dot_t(p[mids:].reshape(mids * k, k), here)
+    up = low[:, :cols] + high[:, cols:]
+    quarter = up[:piece]
+    for r in range(1, 4):
+        quarter = jnp.where(rank == r, up[piece * r : piece * (r + 1)], quarter)
+    quarter = jnp.concatenate([quarter[: piece // 2], quarter[piece // 2 :]], axis=-1).astype(BF16)
+    for i in range(up_ref.shape[0]):
+        up_ref[i] = quarter
 
 
 def first(pos, vectors, basis, child, parent, near_offsets, near_count, leaf_offsets, coupling, ids, total):
@@ -230,8 +231,9 @@
     k = par_ref.shape[1]
     core = pos_ref[1] & 1
     parts = (c0_ref, c1_ref, c2_ref, c3_ref)
+    ids_v[...] = jnp.zeros(ids_v.shape, jnp.int32)
     for b, ref in enumerate(parts):
-        ids_v[b] = ref[k // 2 :].astype(F32).astype(jnp.int32)[:8]
+        ids_v[b : b + 1] = ref[k // 2 :].astype(F32).astype(jnp.int32)[:1]
     copy = pltpu.make_async_copy(ids_v, ids_s, sem)
     copy.start()
     lhs = [ref[: k // 2] for ref in parts]
@@ -240,7 +242,7 @@
     rhs = []
     for b in range(4):
         for s in range(4):
-            u = up_ref[ids_s[b, 0, s]].astype(F32)
+            u = up_ref[ids_s[b, s]].astype(F32)
             rhs += [u[:, :cols], u[:, cols:]]
     top = dot(lhs, jnp.concatenate(rhs, axis=0).astype(BF16))
     top = top.astype(BF16)
@@ -269,8 +271,8 @@
         out_specs=(VMEM, VMEM),
         scratch_shapes=[
             pltpu.VMEM((parent.shape[0], k, c), BF16),
-            pltpu.VMEM((4, 8, 2 * k), jnp.int32),
-            pltpu.SMEM((4, 8, 2 * k), jnp.int32),
+            pltpu.VMEM((8, 2 * k), jnp.int32),
+            pltpu.SMEM((8, 2 * k), jnp.int32),
             pltpu.SemaphoreType.DMA,
         ],
         compiler_params=params(8),

time: 55.5 us -> 55.2 us (level)
  no operation moved by 1% of the time
where the time goes in v4:
time: 55.2 us; the launch traced here: 55 us
  blocking collectives  24.6 us (45%)
  Pallas kernels  15 us (27%)
  starting transfers between devices  9.6 us (17%)
  waiting for transfers between devices  5.63 us (10%)
    all_to_all x1, blocking collectives, shards(): upper = lax.all_to_all(upper, 'leaf', 0, 0)  24.6 us
    pallas_call x1, Pallas kernels, fields(): pl.pallas_call(fields_kernel, out_shape=(out, out), in_specs=[SMEM] * 2 +...  7.78 us
    ppermute x1, starting transfers between devices, shards(): halo_a = lax.ppermute(own, AXES, route)  4.51 us
    ppermute x1, waiting for transfers between devices, shards(): recv = lax.ppermute(send, 'rank', [(i, i ^ 2) for i in range(4)])  4.31 us
    pallas_call x1, Pallas kernels, first(): pl.pallas_call(functools.partial(first_kernel, total=total), out_shape=(j...  3.78 us
    pallas_call x1, Pallas kernels, join(): pl.pallas_call(join_kernel, out_shape=(out, out), in_specs=[SMEM] + [VMEM...  2.4 us
    ppermute x3, starting transfers between devices, shards(): lax.ppermute(coupling[bit], 'rank', [(i, i ^ bit) for i in range(4)])  2.14 us
    ppermute x1, starting transfers between devices, shards(): halo_b = lax.ppermute(halo_a, 'rank', swap)  2 us
  transfers between devices with their start and end apart: 7, of which 3 were waited for; matrix products, arithmetic and copies ran while one was open for 0% of the time, Pallas kernels for 14%

profile of v4, /device:TPU:1, one launch (start us, length us, event | category | flops | bytes accessed | tf_op | source)
XLA Modules:
  0.0 55.0 jit_solution(6158833234050660819)
XLA Ops:
  0.0 0.1 pad_add_fusion.pos_ref
  0.1 3.8 %first.1 = (bf16[64,64,128]{2,1,0:T(8,128)(2,1)S(1)}, bf16[64,8,128]{2,1,0:T(8,128)(2,1)S(1)}, s32[8,64]{1,0:T(8,128)S(1)}, s32[8,64]{1,0:T(8,128)S(1)}, bf16[48...) custom-call(s32[3]{0:T(128)S(1)} %pad_add_fusion.pos_ref, ...), custom_call_target="tpu_custom_call" | custom-call | bytes 9000000 | tf_op jit(solution)/shard_map/first/pallas_call | solution.py:131
  3.9 4.5 %collective-permute-start = (bf16[64,64,128]{2,1,0:T(8,128)(2,1)S(1)}, bf16[64,64,128]{2,1,0:T(8,128)(2,1)S(1)}, u32[]{:S(2)}, u32[]{:S(2)}) collective-permute-start(bf16[64,64,128]{2,1,0:T(8,128)(2,1)S(1)} %get-tuple-element.25.own_ref), channel_id=1, source_target_pairs={{1,4},{3,6},{4,1},{5,8},{6,3},{7,10},{8,5},{9,12},{10,7},{11,14},{... | collective-permute-start | bytes 3145736 | tf_op jit(solution)/shard_map/ppermute | solution.py:384
  8.4 24.6 %all_to_all.5.up_ref = bf16[64,8,128]{2,1,0:T(8,128)(2,1)S(1)} all-to-all(bf16[64,8,128]{2,1,0:T(8,128)(2,1)S(1)} %get-tuple-element.26), channel_id=1, replica_groups=mesh['leaf'=64,'rank'=4] {'leaf'}, dimensions={0} | all-to-all | bytes 262144 | tf_op jit(solution)/shard_map/all_to_all | solution.py:385
  33.0 0.0 collective-permute-done.a_ref
  33.0 2.0 %collective-permute-start.4 = (bf16[64,64,128]{2,1,0:T(8,128)(2,1)S(1)}, bf16[64,64,128]{2,1,0:T(8,128)(2,1)S(1)}, u32[]{:S(2)}, u32[]{:S(2)}) collective-permute-start(bf16[64,64,128]{2,1,0:T(8,128)(2,1)S(1)} %collective-permute-done.a_ref), channel_id=1, source_target_pairs={{0,1},{1,0},{2,3},{3,2},{4,5},{5,4},{6,7},{7,6},{8,9},{9,8},{10,11... | collective-permute-start | bytes 3145736 | tf_op jit(solution)/shard_map/ppermute | solution.py:387
  35.0 0.0 collective-permute-start.1
  35.0 0.4 collective-permute-start.2
  35.4 1.7 %collective-permute-start.3 = (bf16[48,128]{1,0:T(8,128)(2,1)S(1)}, bf16[48,128]{1,0:T(8,128)(2,1)S(1)}, u32[]{:S(2)}, u32[]{:S(2)}) collective-permute-start(bf16[48,128]{1,0:T(8,128)(2,1)S(1)} %get-tuple-element.35), channel_id=1, source_target_pairs={{0,3},{1,2},{2,1},{3,0},{4,7},{5,6},{6,5},{7,4},{8,11},{9,10},{10,... | collective-permute-start | bytes 36872 | tf_op jit(solution)/shard_map/ppermute | solution.py:389
  37.2 0.1 collective-permute-done.4.b_ref
  37.3 0.0 copy-start
  37.3 0.0 copy-start.1
  37.3 0.0 copy-start.2
  37.3 7.8 %fields.1 = (f32[64,64,64]{2,1,0:T(8,128)S(1)}, f32[64,64,64]{2,1,0:T(8,128)S(1)}) custom-call(s32[8,64]{1,0:T(8,128)S(1)} %get-tuple-element.36.near_idx, s32[8,64]{1,0:T(8,128)S(1)} %get-tuple-element.37.leaf_idx, bf16[64,64,128]{2,1,0:T(8,128)(2,1)S(1)} %get-tuple-element.25.own_ref, bf16[64,64,128]{2,1,0:T(8,128)(2,1)S(1)} %collective-permute-done.a_ref, ...), custom_call_target="tpu_custom_call" | custom-call | bytes 24000000 | tf_op jit(solution)/shard_map/fields/pallas_call | solution.py:208
  45.1 0.0 collective-permute-done.1.c1_ref
  45.1 0.0 collective-permute-done.2.c2_ref
  45.1 0.0 collective-permute-done.3.c3_ref
  45.1 0.0 copy-done
  45.1 0.0 copy-done.1
  45.1 0.0 copy-done.2
  45.2 2.4 %join.1 = (bf16[64,16,128]{2,1,0:T(8,128)(2,1)S(1)}, bf16[64,16,128]{2,1,0:T(8,128)(2,1)S(1)}) custom-call(s32[3]{0:T(128)S(1)} %pad_add_fusion.pos_ref, bf16[64,8,128]{2,1,0:T(8,128)(2,1)S(1)} %all_to_all.5.up_ref, bf16[48,128]{1,0:T(8,128)(2,1)S(1)} %get-tuple-element.32.c0_ref, bf16[48,128]{1,0:T(8,128)(2,1)S(1)} %collective-permute-done.1.c1_ref, ...), custom_call_target="tpu_custom_call" | custom-call | bytes 6000000 | tf_op jit(solution)/shard_map/join/pallas_call | solution.py:267
  47.6 0.5 collective-permute-start.5
  48.0 1.2 %collective-permute-done.5.recv_ref = bf16[64,16,128]{2,1,0:T(8,128)(2,1)S(1)} collective-permute-done((bf16[64,16,128]{2,1,0:T(8,128)(2,1)S(1)}, bf16[64,16,128]{2,1,0:T(8,128)(2,1)S(1)}, u32[]{:S(2)}, u32[]{:S(2)}) %collective-permute-start.5) | collective-permute-done | bytes 262176 | tf_op jit(solution)/shard_map/ppermute | solution.py:395
  49.2 0.2 half_sum.1
  49.4 0.5 collective-permute-start.6
  49.9 4.3 %collective-permute-done.6.recv_ref = bf16[32,16,128]{2,1,0:T(8,128)(2,1)S(1)} collective-permute-done((bf16[32,16,128]{2,1,0:T(8,128)(2,1)S(1)}, bf16[32,16,128]{2,1,0:T(8,128)(2,1)S(1)}, u32[]{:S(2)}, u32[]{:S(2)}) %collective-permute-start.6) | collective-permute-done | bytes 131104 | tf_op jit(solution)/shard_map/ppermute | solution.py:397
  54.2 0.8 %last_sum.1 = bf16[64,16,64]{2,1,0:T(8,128)(2,1)} custom-call(f32[64,16,64]{2,1,0:T(8,128)S(1)} %get-tuple-element.43.own_ref, bf16[32,16,128]{2,1,0:T(8,128)(2,1)S(1)} %collective-permute-done.6.recv_ref), custom_call_target="tpu_custom_call" | custom-call | bytes 1500000 | tf_op jit(solution)/shard_map/last_sum/pallas_call | solution.py:320
Async XLA Ops:
  3.9 29.1 %collective-permute-start = (bf16[64,64,128]{2,1,0:T(8,128)(2,1)S(1)}, bf16[64,64,128]{2,1,0:T(8,128)(2,1)S(1)}, u32[]{:S(2)}, u32[]{:S(2)}) collective-permute-start(bf16[64,64,128]{2,1,0:T(8,128)(2,1)S(1)} %get-tuple-element.25.own_ref), channel_id=1, source_target_pairs={{1,4},{3,6},{4,1},{5,8},{6,3},{7,10},{8,5},{9,12},{10,7},{11,14},{... | collective-permute-start | bytes 3145736 | tf_op jit(solution)/shard_map/ppermute | solution.py:384
  33.0 4.3 %collective-permute-start.4 = (bf16[64,64,128]{2,1,0:T(8,128)(2,1)S(1)}, bf16[64,64,128]{2,1,0:T(8,128)(2,1)S(1)}, u32[]{:S(2)}, u32[]{:S(2)}) collective-permute-start(bf16[64,64,128]{2,1,0:T(8,128)(2,1)S(1)} %collective-permute-done.a_ref), channel_id=1, source_target_pairs={{0,1},{1,0},{2,3},{3,2},{4,5},{5,4},{6,7},{7,6},{8,9},{9,8},{10,11... | collective-permute-start | bytes 3145736 | tf_op jit(solution)/shard_map/ppermute | solution.py:387
  35.0 10.1 %collective-permute-start.1 = (bf16[48,128]{1,0:T(8,128)(2,1)S(1)}, bf16[48,128]{1,0:T(8,128)(2,1)S(1)}, u32[]{:S(2)}, u32[]{:S(2)}) collective-permute-start(bf16[48,128]{1,0:T(8,128)(2,1)S(1)} %get-tuple-element.33), channel_id=1, source_target_pairs={{0,1},{1,0},{2,3},{3,2},{4,5},{5,4},{6,7},{7,6},{8,9},{9,8},{10,11... | collective-permute-start | bytes 36872 | tf_op jit(solution)/shard_map/ppermute | solution.py:389
  35.0 10.1 %collective-permute-start.2 = (bf16[48,128]{1,0:T(8,128)(2,1)S(1)}, bf16[48,128]{1,0:T(8,128)(2,1)S(1)}, u32[]{:S(2)}, u32[]{:S(2)}) collective-permute-start(bf16[48,128]{1,0:T(8,128)(2,1)S(1)} %get-tuple-element.34), channel_id=1, source_target_pairs={{0,2},{1,3},{2,0},{3,1},{4,6},{5,7},{6,4},{7,5},{8,10},{9,11},{10,... | collective-permute-start | bytes 36872 | tf_op jit(solution)/shard_map/ppermute | solution.py:389
  35.4 9.7 %collective-permute-start.3 = (bf16[48,128]{1,0:T(8,128)(2,1)S(1)}, bf16[48,128]{1,0:T(8,128)(2,1)S(1)}, u32[]{:S(2)}, u32[]{:S(2)}) collective-permute-start(bf16[48,128]{1,0:T(8,128)(2,1)S(1)} %get-tuple-element.35), channel_id=1, source_target_pairs={{0,3},{1,2},{2,1},{3,0},{4,7},{5,6},{6,5},{7,4},{8,11},{9,10},{10,... | collective-permute-start | bytes 36872 | tf_op jit(solution)/shard_map/ppermute | solution.py:389
  37.3 7.8 %copy-start = (bf16[64,64,64]{2,1,0:T(8,128)(2,1)S(1)}, bf16[64,64,64]{2,1,0:T(8,128)(2,1)}, u32[]{:S(2)}) copy-start(bf16[64,64,64]{2,1,0:T(8,128)(2,1)} %basis_ref.1) | copy-start | bytes 1572868
  37.3 7.8 %copy-start.1 = (bf16[64,64,64]{2,1,0:T(8,128)(2,1)S(1)}, bf16[64,64,64]{2,1,0:T(8,128)(2,1)}, u32[]{:S(2)}) copy-start(bf16[64,64,64]{2,1,0:T(8,128)(2,1)} %child_ref.1) | copy-start | bytes 1572868
  37.3 7.8 %copy-start.2 = (bf16[8,64,64]{2,1,0:T(8,128)(2,1)S(1)}, bf16[8,64,64]{2,1,0:T(8,128)(2,1)}, u32[]{:S(2)}) copy-start(bf16[8,64,64]{2,1,0:T(8,128)(2,1)} %par_ref.1) | copy-start | bytes 196612
  47.6 1.6 %collective-permute-start.5 = (bf16[64,16,128]{2,1,0:T(8,128)(2,1)S(1)}, bf16[64,16,128]{2,1,0:T(8,128)(2,1)S(1)}, u32[]{:S(2)}, u32[]{:S(2)}) collective-permute-start(bf16[64,16,128]{2,1,0:T(8,128)(2,1)S(1)} %get-tuple-element.42), channel_id=1, source_target_pairs={{0,1},{1,0},{2,3},{3,2},{4,5},{5,4},{6,7},{7,6},{8,9},{9,8},{10,11... | collective-permute-start | bytes 786440 | tf_op jit(solution)/shard_map/ppermute | solution.py:395
  49.4 4.8 %collective-permute-start.6 = (bf16[32,16,128]{2,1,0:T(8,128)(2,1)S(1)}, bf16[32,16,128]{2,1,0:T(8,128)(2,1)S(1)}, u32[]{:S(2)}, u32[]{:S(2)}) collective-permute-start(bf16[32,16,128]{2,1,0:T(8,128)(2,1)S(1)} %get-tuple-element.44), channel_id=1, source_target_pairs={{0,2},{1,3},{2,0},{3,1},{4,6},{5,7},{6,4},{7,5},{8,10},{9,11},{10,... | collective-permute-start | bytes 393224 | tf_op jit(solution)/shard_map/ppermute | solution.py:397

commit v5 on v4

--- a/solution.py
+++ b/solution.py
@@ -156,7 +156,7 @@
 
 
 CHUNK = 8
-AHEAD = 3
+AHEAD = 2
 
 
 def fields_kernel(

time: 55.2 us -> 56.7 us (1.027)
  Pallas kernels: 15 us -> 16.5 us
    pallas_call x1, Pallas kernels: 7.78 us -> 9.25 us  [fields(): pl.pallas_call(fields_kernel, out_shape=(out, out), in_specs=[SMEM] * 2 +...]
  transfers between devices with their start and end apart: 7 -> 7, of which waited for: 3 -> 3; matrix products, arithmetic and copies ran while one was open for 0% -> 0% of each run, Pallas kernels for 14% -> 16%
where the time goes in v5:
time: 56.7 us; the launch traced here: 56.5 us
  blocking collectives  24.6 us (43%)
  Pallas kernels  16.5 us (29%)
  starting transfers between devices  9.59 us (17%)
  waiting for transfers between devices  5.63 us (10%)
    all_to_all x1, blocking collectives, shards(): upper = lax.all_to_all(upper, 'leaf', 0, 0)  24.6 us
    pallas_call x1, Pallas kernels, fields(): pl.pallas_call(fields_kernel, out_shape=(out, out), in_specs=[SMEM] * 2 +...  9.25 us
    ppermute x1, starting transfers between devices, shards(): halo_a = lax.ppermute(own, AXES, route)  4.51 us
    ppermute x1, waiting for transfers between devices, shards(): recv = lax.ppermute(send, 'rank', [(i, i ^ 2) for i in range(4)])  4.31 us
    pallas_call x1, Pallas kernels, first(): pl.pallas_call(functools.partial(first_kernel, total=total), out_shape=(j...  3.78 us
    pallas_call x1, Pallas kernels, join(): pl.pallas_call(join_kernel, out_shape=(out, out), in_specs=[SMEM] + [VMEM...  2.4 us
    ppermute x3, starting transfers between devices, shards(): lax.ppermute(coupling[bit], 'rank', [(i, i ^ bit) for i in range(4)])  2.14 us
    ppermute x1, starting transfers between devices, shards(): halo_b = lax.ppermute(halo_a, 'rank', swap)  2 us
  transfers between devices with their start and end apart: 7, of which 3 were waited for; matrix products, arithmetic and copies ran while one was open for 0% of the time, Pallas kernels for 16%

profile of v5, /device:TPU:1, one launch (start us, length us, event | category | flops | bytes accessed | tf_op | source)
XLA Modules:
  0.0 56.5 jit_solution(4323290032284319030)
XLA Ops:
  0.0 0.1 pad_add_fusion.pos_ref
  0.1 3.8 %first.1 = (bf16[64,64,128]{2,1,0:T(8,128)(2,1)S(1)}, bf16[64,8,128]{2,1,0:T(8,128)(2,1)S(1)}, s32[8,64]{1,0:T(8,128)S(1)}, s32[8,64]{1,0:T(8,128)S(1)}, bf16[48...) custom-call(s32[3]{0:T(128)S(1)} %pad_add_fusion.pos_ref, ...), custom_call_target="tpu_custom_call" | custom-call | bytes 9000000 | tf_op jit(solution)/shard_map/first/pallas_call | solution.py:131
  3.9 4.5 %collective-permute-start = (bf16[64,64,128]{2,1,0:T(8,128)(2,1)S(1)}, bf16[64,64,128]{2,1,0:T(8,128)(2,1)S(1)}, u32[]{:S(2)}, u32[]{:S(2)}) collective-permute-start(bf16[64,64,128]{2,1,0:T(8,128)(2,1)S(1)} %get-tuple-element.25.own_ref), channel_id=1, source_target_pairs={{1,4},{3,6},{4,1},{5,8},{6,3},{7,10},{8,5},{9,12},{10,7},{11,14},{... | collective-permute-start | bytes 3145736 | tf_op jit(solution)/shard_map/ppermute | solution.py:384
  8.4 24.6 %all_to_all.5.up_ref = bf16[64,8,128]{2,1,0:T(8,128)(2,1)S(1)} all-to-all(bf16[64,8,128]{2,1,0:T(8,128)(2,1)S(1)} %get-tuple-element.26), channel_id=1, replica_groups=mesh['leaf'=64,'rank'=4] {'leaf'}, dimensions={0} | all-to-all | bytes 262144 | tf_op jit(solution)/shard_map/all_to_all | solution.py:385
  33.0 0.0 collective-permute-done.a_ref
  33.0 2.0 %collective-permute-start.4 = (bf16[64,64,128]{2,1,0:T(8,128)(2,1)S(1)}, bf16[64,64,128]{2,1,0:T(8,128)(2,1)S(1)}, u32[]{:S(2)}, u32[]{:S(2)}) collective-permute-start(bf16[64,64,128]{2,1,0:T(8,128)(2,1)S(1)} %collective-permute-done.a_ref), channel_id=1, source_target_pairs={{0,1},{1,0},{2,3},{3,2},{4,5},{5,4},{6,7},{7,6},{8,9},{9,8},{10,11... | collective-permute-start | bytes 3145736 | tf_op jit(solution)/shard_map/ppermute | solution.py:387
  35.0 0.0 collective-permute-start.1
  35.0 0.4 collective-permute-start.2
  35.4 1.7 %collective-permute-start.3 = (bf16[48,128]{1,0:T(8,128)(2,1)S(1)}, bf16[48,128]{1,0:T(8,128)(2,1)S(1)}, u32[]{:S(2)}, u32[]{:S(2)}) collective-permute-start(bf16[48,128]{1,0:T(8,128)(2,1)S(1)} %get-tuple-element.35), channel_id=1, source_target_pairs={{0,3},{1,2},{2,1},{3,0},{4,7},{5,6},{6,5},{7,4},{8,11},{9,10},{10,... | collective-permute-start | bytes 36872 | tf_op jit(solution)/shard_map/ppermute | solution.py:389
  37.2 0.1 collective-permute-done.4.b_ref
  37.3 0.0 copy-start
  37.3 0.0 copy-start.1
  37.3 0.0 copy-start.2
  37.3 9.2 %fields.1 = (f32[64,64,64]{2,1,0:T(8,128)S(1)}, f32[64,64,64]{2,1,0:T(8,128)S(1)}) custom-call(s32[8,64]{1,0:T(8,128)S(1)} %get-tuple-element.36.near_idx, s32[8,64]{1,0:T(8,128)S(1)} %get-tuple-element.37.leaf_idx, bf16[64,64,128]{2,1,0:T(8,128)(2,1)S(1)} %get-tuple-element.25.own_ref, bf16[64,64,128]{2,1,0:T(8,128)(2,1)S(1)} %collective-permute-done.a_ref, ...), custom_call_target="tpu_custom_call" | custom-call | bytes 24000000 | tf_op jit(solution)/shard_map/fields/pallas_call | solution.py:208
  46.6 0.0 collective-permute-done.1.c1_ref
  46.6 0.0 collective-permute-done.2.c2_ref
  46.6 0.0 collective-permute-done.3.c3_ref
  46.6 0.0 copy-done
  46.6 0.0 copy-done.1
  46.6 0.0 copy-done.2
  46.6 2.4 %join.1 = (bf16[64,16,128]{2,1,0:T(8,128)(2,1)S(1)}, bf16[64,16,128]{2,1,0:T(8,128)(2,1)S(1)}) custom-call(s32[3]{0:T(128)S(1)} %pad_add_fusion.pos_ref, bf16[64,8,128]{2,1,0:T(8,128)(2,1)S(1)} %all_to_all.5.up_ref, bf16[48,128]{1,0:T(8,128)(2,1)S(1)} %get-tuple-element.32.c0_ref, bf16[48,128]{1,0:T(8,128)(2,1)S(1)} %collective-permute-done.1.c1_ref, ...), custom_call_target="tpu_custom_call" | custom-call | bytes 6000000 | tf_op jit(solution)/shard_map/join/pallas_call | solution.py:267
  49.0 0.5 collective-permute-start.5
  49.5 1.2 %collective-permute-done.5.recv_ref = bf16[64,16,128]{2,1,0:T(8,128)(2,1)S(1)} collective-permute-done((bf16[64,16,128]{2,1,0:T(8,128)(2,1)S(1)}, bf16[64,16,128]{2,1,0:T(8,128)(2,1)S(1)}, u32[]{:S(2)}, u32[]{:S(2)}) %collective-permute-start.5) | collective-permute-done | bytes 262176 | tf_op jit(solution)/shard_map/ppermute | solution.py:395
  50.6 0.2 half_sum.1
  50.9 0.5 collective-permute-start.6
  51.4 4.3 %collective-permute-done.6.recv_ref = bf16[32,16,128]{2,1,0:T(8,128)(2,1)S(1)} collective-permute-done((bf16[32,16,128]{2,1,0:T(8,128)(2,1)S(1)}, bf16[32,16,128]{2,1,0:T(8,128)(2,1)S(1)}, u32[]{:S(2)}, u32[]{:S(2)}) %collective-permute-start.6) | collective-permute-done | bytes 131104 | tf_op jit(solution)/shard_map/ppermute | solution.py:397
  55.7 0.8 %last_sum.1 = bf16[64,16,64]{2,1,0:T(8,128)(2,1)} custom-call(f32[64,16,64]{2,1,0:T(8,128)S(1)} %get-tuple-element.43.own_ref, bf16[32,16,128]{2,1,0:T(8,128)(2,1)S(1)} %collective-permute-done.6.recv_ref), custom_call_target="tpu_custom_call" | custom-call | bytes 1500000 | tf_op jit(solution)/shard_map/last_sum/pallas_call | solution.py:320
Async XLA Ops:
  3.9 29.1 %collective-permute-start = (bf16[64,64,128]{2,1,0:T(8,128)(2,1)S(1)}, bf16[64,64,128]{2,1,0:T(8,128)(2,1)S(1)}, u32[]{:S(2)}, u32[]{:S(2)}) collective-permute-start(bf16[64,64,128]{2,1,0:T(8,128)(2,1)S(1)} %get-tuple-element.25.own_ref), channel_id=1, source_target_pairs={{1,4},{3,6},{4,1},{5,8},{6,3},{7,10},{8,5},{9,12},{10,7},{11,14},{... | collective-permute-start | bytes 3145736 | tf_op jit(solution)/shard_map/ppermute | solution.py:384
  33.0 4.3 %collective-permute-start.4 = (bf16[64,64,128]{2,1,0:T(8,128)(2,1)S(1)}, bf16[64,64,128]{2,1,0:T(8,128)(2,1)S(1)}, u32[]{:S(2)}, u32[]{:S(2)}) collective-permute-start(bf16[64,64,128]{2,1,0:T(8,128)(2,1)S(1)} %collective-permute-done.a_ref), channel_id=1, source_target_pairs={{0,1},{1,0},{2,3},{3,2},{4,5},{5,4},{6,7},{7,6},{8,9},{9,8},{10,11... | collective-permute-start | bytes 3145736 | tf_op jit(solution)/shard_map/ppermute | solution.py:387
  35.0 11.5 %collective-permute-start.1 = (bf16[48,128]{1,0:T(8,128)(2,1)S(1)}, bf16[48,128]{1,0:T(8,128)(2,1)S(1)}, u32[]{:S(2)}, u32[]{:S(2)}) collective-permute-start(bf16[48,128]{1,0:T(8,128)(2,1)S(1)} %get-tuple-element.33), channel_id=1, source_target_pairs={{0,1},{1,0},{2,3},{3,2},{4,5},{5,4},{6,7},{7,6},{8,9},{9,8},{10,11... | collective-permute-start | bytes 36872 | tf_op jit(solution)/shard_map/ppermute | solution.py:389
  35.0 11.6 %collective-permute-start.2 = (bf16[48,128]{1,0:T(8,128)(2,1)S(1)}, bf16[48,128]{1,0:T(8,128)(2,1)S(1)}, u32[]{:S(2)}, u32[]{:S(2)}) collective-permute-start(bf16[48,128]{1,0:T(8,128)(2,1)S(1)} %get-tuple-element.34), channel_id=1, source_target_pairs={{0,2},{1,3},{2,0},{3,1},{4,6},{5,7},{6,4},{7,5},{8,10},{9,11},{10,... | collective-permute-start | bytes 36872 | tf_op jit(solution)/shard_map/ppermute | solution.py:389
  35.4 11.2 %collective-permute-start.3 = (bf16[48,128]{1,0:T(8,128)(2,1)S(1)}, bf16[48,128]{1,0:T(8,128)(2,1)S(1)}, u32[]{:S(2)}, u32[]{:S(2)}) collective-permute-start(bf16[48,128]{1,0:T(8,128)(2,1)S(1)} %get-tuple-element.35), channel_id=1, source_target_pairs={{0,3},{1,2},{2,1},{3,0},{4,7},{5,6},{6,5},{7,4},{8,11},{9,10},{10,... | collective-permute-start | bytes 36872 | tf_op jit(solution)/shard_map/ppermute | solution.py:389
  37.3 9.3 %copy-start = (bf16[64,64,64]{2,1,0:T(8,128)(2,1)S(1)}, bf16[64,64,64]{2,1,0:T(8,128)(2,1)}, u32[]{:S(2)}) copy-start(bf16[64,64,64]{2,1,0:T(8,128)(2,1)} %basis_ref.1) | copy-start | bytes 1572868
  37.3 9.3 %copy-start.1 = (bf16[64,64,64]{2,1,0:T(8,128)(2,1)S(1)}, bf16[64,64,64]{2,1,0:T(8,128)(2,1)}, u32[]{:S(2)}) copy-start(bf16[64,64,64]{2,1,0:T(8,128)(2,1)} %child_ref.1) | copy-start | bytes 1572868
  37.3 9.3 %copy-start.2 = (bf16[8,64,64]{2,1,0:T(8,128)(2,1)S(1)}, bf16[8,64,64]{2,1,0:T(8,128)(2,1)}, u32[]{:S(2)}) copy-start(bf16[8,64,64]{2,1,0:T(8,128)(2,1)} %par_ref.1) | copy-start | bytes 196612
  49.0 1.6 %collective-permute-start.5 = (bf16[64,16,128]{2,1,0:T(8,128)(2,1)S(1)}, bf16[64,16,128]{2,1,0:T(8,128)(2,1)S(1)}, u32[]{:S(2)}, u32[]{:S(2)}) collective-permute-start(bf16[64,16,128]{2,1,0:T(8,128)(2,1)S(1)} %get-tuple-element.42), channel_id=1, source_target_pairs={{0,1},{1,0},{2,3},{3,2},{4,5},{5,4},{6,7},{7,6},{8,9},{9,8},{10,11... | collective-permute-start | bytes 786440 | tf_op jit(solution)/shard_map/ppermute | solution.py:395
  50.9 4.8 %collective-permute-start.6 = (bf16[32,16,128]{2,1,0:T(8,128)(2,1)S(1)}, bf16[32,16,128]{2,1,0:T(8,128)(2,1)S(1)}, u32[]{:S(2)}, u32[]{:S(2)}) collective-permute-start(bf16[32,16,128]{2,1,0:T(8,128)(2,1)S(1)} %get-tuple-element.44), channel_id=1, source_target_pairs={{0,2},{1,3},{2,0},{3,1},{4,6},{5,7},{6,4},{7,5},{8,10},{9,11},{10,... | collective-permute-start | bytes 393224 | tf_op jit(solution)/shard_map/ppermute | solution.py:397
